TPU v7x, 768 devices: a whole 4x8x12 slice. The times are simulated.
768 devices in a mesh: gx: 8 (over x, z_hi), gy: 16 (over y, core), gz: 6 (over z_lo).
Axes of the slice: x: 4, y: 8, z: 12 (z_hi: 2, z_lo: 6; z = z_hi * 6 + z_lo), core: 2. Of those that a mesh axis runs over, the one named last changes fastest.
Arguments:
- positions: float32 [48, 16, 16, 3, 128], P(('gx', 'gz'), 'gy'), may hold values from 0 to 1
- masses: float32 [48, 16, 16, 128], P(('gx', 'gz'), 'gy'), may hold values from 0.2 to 2
- velocities: float32 [48, 16, 16, 3, 128], P(('gx', 'gz'), 'gy'), may hold values from -6 to 6
- tile_counts: int32 [48, 16, 16], P(('gx', 'gz'), 'gy'), may hold values from 32 to 128
- neighbour_list: int32 [48, 16, 16, 6], P(('gx', 'gz'), 'gy'), may hold values from 0 to 143, as said below
Outputs:
- kicked: float32 [48, 16, 16, 3, 128], P(('gx', 'gz'), 'gy')
Inputs may be any that keep to these rules, and one draw needn't show every extreme that they name: `neighbour_list`: each entry is ((dx + 1) * 3 + dy + 1) * 16 + (t + dz) mod 16 for the tile t it belongs to, dx, dy, dz each in -1, 0, 1; the 6 entries of one tile name distinct shell tiles.
All inputs are finite; a program needn't handle non-finite values.
Results may differ from a plain program's by a relative error of at most 0.0003.
Values sent between devices are 32-bit elements; how exact they have to be, the bound alone decides.
No kernel may reach another device: no remote copies, remote signals or barrier semaphores. Data moves between devices by JAX's collectives and lax.ppermute only.
A program may use at most 64 MiB of HBM per device.

v0:
```python
import functools

import jax
import jax.numpy as jnp
import ml_dtypes
import numpy as np
from jax import lax
from jax.experimental import pallas as pl
from jax.experimental.pallas import tpu as pltpu
from jax.sharding import PartitionSpec as P

CX = 2
CY = 6
NZ = 1024
TZ = 16
NB = 6
NX = 96
NY = 96
PX = 48
PY = 16
CELLS = NZ // TZ
BLOCK = NZ // PY
HALF = BLOCK // 2

smoothing = 0.1
screening = 0.01
split_scale = 2.0
softening = 0.05
long_kick = 1.0
short_kick = 0.05

f32 = jnp.float32
bf16 = jnp.bfloat16


def halves(table):
    high = table.astype(np.float32).astype(ml_dtypes.bfloat16)
    low = (table - high.astype(np.float64)).astype(np.float32).astype(ml_dtypes.bfloat16)
    return high, low


def real_basis(length, run):
    cells = np.arange(length)[:, None]
    wave = np.arange(length // 2)
    angle = 2 * np.pi * (cells * wave[None] % length) / length
    cosine = np.cos(angle) * np.sqrt(2 / length)
    sine = np.sin(angle) * np.sqrt(2 / length)
    step = np.sin(2 * np.pi * wave / length)
    cos_slope = sine * step
    sin_slope = -cosine * step
    cosine[:, 0] = np.sqrt(1 / length)
    sine[:, 0] = np.where(cells[:, 0] % 2 == 0, 1.0, -1.0) * np.sqrt(1 / length)
    cos_slope[:, 0] = 0
    sin_slope[:, 0] = 0
    kappa_cos = 4 * np.sin(np.pi * wave / length) ** 2
    kappa_sin = kappa_cos.copy()
    kappa_sin[0] = 4.0

    def laid(first, second):
        shape = first.shape[:-1] + (-1, 1, run)
        return np.concatenate([first.reshape(shape), second.reshape(shape)], axis=-2).reshape(
            first.shape[:-1] + (length,)
        )

    return (
        laid(cosine, sine),
        laid(cos_slope, sin_slope),
        laid(kappa_cos, kappa_sin),
        laid(-step, step),
    )


@functools.lru_cache(None)
def tables():
    basis_z, _, kappa_z, sine_z = real_basis(NZ, HALF)
    basis_x, slope_x, kappa_x, _ = real_basis(NX, 1)
    basis_y, slope_y, kappa_y, _ = real_basis(NY, 1)
    out = {}
    out["fwd_z"] = halves(basis_z)
    out["inv_z"] = halves(basis_z.T)
    pad_y = np.zeros((NY, PY, 8))
    pad_y[:, :, :CY] = basis_y.T.reshape(NY, PY, CY)
    out["fwd_y"] = halves(pad_y.reshape(NY, PY * 8))
    out["fwd_x"] = halves(basis_x.reshape(PX, CX, NX).transpose(2, 1, 0).reshape(NX, CX * PX))
    both = np.stack([slope_x.reshape(PX, CX, NX), basis_x.reshape(PX, CX, NX)], axis=1)
    out["inv_x"] = halves(both.reshape(PX * 2 * CX, NX))

    def rows_y(table):
        padded = np.zeros((2, PY, 8, PX))
        padded[:, :, :CY] = table.reshape(PY, CY, PX, 2).transpose(3, 0, 1, 2)
        return padded.reshape(2 * PY * 8, PX)

    out["inv_y"] = halves(np.concatenate([rows_y(basis_y), rows_y(slope_y)], axis=0))
    out["kappa_x"] = kappa_x[:, None].astype(np.float32)
    out["kappa_y"] = np.repeat(kappa_y.reshape(PX, 2), BLOCK, axis=1).astype(np.float32)
    out["kappa_z"] = np.tile(kappa_z.reshape(PY, BLOCK), (1, 2)).astype(np.float32)
    out["sine_z"] = np.tile(sine_z.reshape(PY, BLOCK), (1, 2)).astype(np.float32)
    return out


def split(value):
    high = value.astype(bf16)
    return high, (value - high.astype(f32)).astype(bf16)


def dot(left, right):
    return lax.dot_general(left, right, (((1,), (0,)), ((), ())), preferred_element_type=f32)


def dot_t(left, right):
    return lax.dot_general(left, right, (((1,), (1,)), ((), ())), preferred_element_type=f32)


def table_dot(high_ref, low_ref, value):
    high, low = split(value)
    return dot(high_ref[...], high) + dot(high_ref[...], low) + dot(low_ref[...], high)


def dot_table(value, high_ref, low_ref):
    rows = value.shape[0]
    high, low = split(value)
    both = dot(jnp.concatenate([high, low], axis=0), high_ref[...])
    return both[:rows] + both[rows:] + dot(high, low_ref[...])


def iota(shape, dim):
    return lax.broadcasted_iota(jnp.int32, shape, dim)


def plane_weights(pos_ref, tile):
    row = iota((16, 128), 0)
    row_x = (row >> 3).astype(f32)
    row_y = (row & 7).astype(f32)
    x = jnp.clip(pos_ref[0, tile : tile + 1, :] * CX - 0.5, 0.0, 1.0)
    y = jnp.clip(pos_ref[1, tile : tile + 1, :] * CY - 0.5, 0.0, CY - 1.0)
    return (1.0 - jnp.abs(x - row_x)) * jnp.maximum(1.0 - jnp.abs(y - row_y), 0.0)


def depth_weights(pos_ref, tile):
    z = (tile + pos_ref[2, tile : tile + 1, :]) * CELLS - 0.5 - (tile * CELLS - CELLS // 2)
    return jnp.maximum(1.0 - jnp.abs(z - iota((128, 128), 0).astype(f32)), 0.0)


def deposit_kernel(counts, pos_ref, mass_ref, high_ref, low_ref, out_ref):
    slot = iota((1, 128), 1)
    windows = []
    for tile in range(TZ):
        mass = jnp.where(slot < counts[0, tile], mass_ref[tile : tile + 1, :], 0.0)
        flat_high, flat_low = split(plane_weights(pos_ref, tile) * mass)
        deep_high, deep_low = split(depth_weights(pos_ref, tile))
        windows.append(
            dot_t(flat_high, deep_high) + dot_t(flat_high, deep_low) + dot_t(flat_low, deep_high)
        )
    even = jnp.concatenate(windows[0::2], axis=1)
    odd = jnp.concatenate(windows[1::2], axis=1)
    density = pltpu.roll(even, NZ - CELLS // 2, 1) + pltpu.roll(odd, CELLS // 2, 1)
    modes = dot_table(density, high_ref, low_ref)
    first = iota((8, 128), 1) < BLOCK
    for pair in range(PY // 2):
        lanes = slice(128 * pair, 128 * (pair + 1))
        near = modes[:8, lanes]
        far = modes[8:, lanes]
        out_ref[2 * pair] = jnp.where(first, near, pltpu.roll(far, BLOCK, 1))
        out_ref[2 * pair + 1] = jnp.where(first, pltpu.roll(near, BLOCK, 1), far)


def forward_y_kernel(in_ref, high_ref, low_ref, out_ref):
    out_ref[...] = table_dot(high_ref, low_ref, in_ref[...])


def solve_x_kernel(
    in_ref, fwd_high, fwd_low, inv_high, inv_low, kappa_x, kappa_y, kappa_z, out_ref
):
    at_x = lax.axis_index(("gx", "gz"))
    at_y = lax.axis_index("gy")
    first = iota((PX, 128), 1) < BLOCK
    wave_a = in_ref[pl.ds(0, PX, stride=2), :]
    wave_b = in_ref[pl.ds(1, PX, stride=2), :]
    cells_0 = jnp.where(first, wave_a, pltpu.roll(wave_b, BLOCK, 1))
    cells_1 = jnp.where(first, pltpu.roll(wave_a, BLOCK, 1), wave_b)
    spectrum = table_dot(fwd_high, fwd_low, jnp.concatenate([cells_0, cells_1], axis=0))
    kappa_sum = kappa_x[...] + (kappa_y[pl.ds(at_x, 1), :] + kappa_z[pl.ds(at_y, 1), :])
    potential = spectrum * (-jnp.exp(-smoothing * kappa_sum) / (kappa_sum + screening))
    out_ref[...] = table_dot(inv_high, inv_low, potential)


def inverse_y_kernel(in_ref, high_ref, low_ref, out_ref):
    rows = PY * 8
    first = iota((rows, 128), 1) < BLOCK
    fields = [in_ref[pl.ds(at, PX, stride=4), :] for at in range(4)]
    slope_x_high, slope_x_low = split(jnp.concatenate(fields[:2], axis=1))
    phi_high, phi_low = split(jnp.concatenate(fields[2:], axis=1))

    def product(table_rows, high, low):
        a = high_ref[table_rows, :]
        return dot(a, high) + dot(a, low) + dot(low_ref[table_rows, :], high)

    force_x = product(slice(0, 2 * rows), slope_x_high, slope_x_low)
    others = product(slice(0, 4 * rows), phi_high, phi_low)
    for field, value in enumerate((force_x, others[2 * rows :], others[: 2 * rows])):
        cos_0, cos_1 = value[:rows, :128], value[:rows, 128:]
        sin_0, sin_1 = value[rows:, :128], value[rows:, 128:]
        cell_0 = cos_0 + pltpu.roll(sin_0, BLOCK, 1)
        cell_1 = pltpu.roll(cos_1, BLOCK, 1) + sin_1
        merged = jnp.where(first, cell_0, cell_1)
        out_ref[:, 8 * field : 8 * field + 8, :] = merged.reshape(PY, 8, 128)


def kick_kernel(
    counts, in_ref, pos_ref, vel_ref, short_ref, high_ref, low_ref, sine_ref, out_ref
):
    first = iota((24, 128), 1) < BLOCK
    cosines = (iota((8, 128), 1) & (BLOCK - 1)) < HALF
    slot = iota((1, 128), 1)

    def block(at):
        value = in_ref[at]
        phi = value[16:24]
        turned = jnp.where(
            cosines, pltpu.roll(phi, 128 - HALF, 1), pltpu.roll(phi, HALF, 1)
        )
        return jnp.concatenate([value[:16], turned * sine_ref[at : at + 1, :]], axis=0)

    near, far = [], []
    for pair in range(PY // 2):
        a, b = block(2 * pair), block(2 * pair + 1)
        near.append(jnp.where(first, a, pltpu.roll(b, BLOCK, 1)))
        far.append(jnp.where(first, pltpu.roll(a, BLOCK, 1), b))
    modes = jnp.concatenate(
        [jnp.concatenate(near, axis=1), jnp.concatenate(far, axis=1)], axis=0
    )
    forces = dot_table(modes, high_ref, low_ref)
    shifted = (
        pltpu.roll(forces, CELLS // 2, 1),
        pltpu.roll(forces, NZ - CELLS // 2, 1),
    )
    for tile in range(TZ):
        start = 128 * (tile // 2)
        window = shifted[tile % 2][:, start : start + 128]
        high, low = split(window)
        deep_high, deep_low = split(depth_weights(pos_ref, tile))
        both = dot(jnp.concatenate([high, low], axis=0), deep_high)
        picked = both[:48] + both[48:] + dot(high, deep_low)
        flat = plane_weights(pos_ref, tile)
        live = slot < counts[0, tile]
        for comp in range(3):
            at = 8 * comp
            total = flat[:8] * picked[at : at + 8] + flat[8:] * picked[24 + at : 32 + at]
            long_accel = jnp.sum(total, axis=0, keepdims=True)
            kick = long_kick * long_accel + short_kick * short_ref[comp, tile : tile + 1, :]
            out_ref[comp, tile : tile + 1, :] = vel_ref[comp, tile : tile + 1, :] + jnp.where(
                live, kick, 0.0
            )


def short_kernel(listed, own_ref, left_ref, mid_ref, right_ref, out_ref, shell, sums):
    for at, ref in enumerate((left_ref, mid_ref, right_ref)):
        for dx in range(3):
            shell[3 * dx + at] = ref[dx]

    def one_tile(tile, carry):
        rows = [own_ref[comp, pl.ds(tile, 1), :] for comp in range(3)]
        columns = jnp.concatenate(rows + [jnp.zeros((5, 128), f32)], axis=0).T
        sources = []
        for entry in range(NB):
            code = listed[entry, tile]
            group = code >> 4
            layer = code & (TZ - 1)
            step_x = (group * 11) >> 5
            step_y = group - 3 * step_x
            step_z = (layer - tile + 1) & (TZ - 1)
            shifts = [(step - 1).astype(f32) for step in (step_x, step_y, step_z)]
            source = [shell[group, comp, pl.ds(layer, 1), :] for comp in range(4)]
            sources.append([source[comp] + shifts[comp] for comp in range(3)] + [source[3]])
        for chunk in range(16):
            part = slice(8 * chunk, 8 * chunk + 8)
            own = [jnp.broadcast_to(columns[part, comp : comp + 1], (8, 128)) for comp in range(3)]
            totals = [None] * 3
            for x, y, z, mass in sources:
                apart = [x - own[0], y - own[1], z - own[2]]
                square = apart[0] * apart[0] + apart[1] * apart[1] + apart[2] * apart[2]
                root = lax.rsqrt(square + softening)
                strength = (mass * jnp.exp(square * (-1.0 / split_scale))) * (root * root * root)
                for comp in range(3):
                    term = strength * apart[comp]
                    totals[comp] = term if totals[comp] is None else totals[comp] + term
            for comp in range(3):
                sums[128 * comp + 8 * chunk : 128 * comp + 8 * chunk + 8, :] = totals[comp]
        ones = jnp.ones((8, 128), bf16)
        high, low = split(sums[...])
        total = dot_t(ones, high) + dot_t(ones, low)
        for comp in range(3):
            out_ref[comp, pl.ds(tile, 1), :] = total[:1, 128 * comp : 128 * comp + 128]
        return carry

    lax.fori_loop(0, TZ, one_tile, 0)


def call(kernel, shape, operands, smem=0, scratch=(), cost=None):
    specs = [pl.BlockSpec(memory_space=pltpu.SMEM)] * smem
    specs += [pl.BlockSpec(memory_space=pltpu.VMEM)] * (len(operands) - smem)
    return pl.pallas_call(
        kernel,
        out_shape=jax.ShapeDtypeStruct(shape, f32),
        in_specs=specs,
        out_specs=pl.BlockSpec(memory_space=pltpu.VMEM),
        scratch_shapes=scratch,
        cost_estimate=cost,
        compiler_params=pltpu.CompilerParams(vmem_limit_bytes=24 << 20),
    )(*operands)


def exchange(value, axis):
    return lax.all_to_all(value, axis, split_axis=0, concat_axis=0, tiled=True)


def shift(value, axis, count, step):
    return lax.ppermute(value, axis, [(i, (i + step) % count) for i in range(count)])


def shards(positions, masses, velocities, tile_counts, neighbour_list):
    t = tables()
    wide = ("gx", "gz")
    position = jnp.transpose(positions[0, 0], (1, 0, 2))
    velocity = jnp.transpose(velocities[0, 0], (1, 0, 2))
    mass = masses[0, 0]
    counts = tile_counts[0]
    listed = jnp.transpose(neighbour_list[0, 0], (1, 0))

    modes = call(deposit_kernel, (PY, 8, 128), (counts, position, mass, *t["fwd_z"]), smem=1)

    live = lax.broadcasted_iota(jnp.int32, (TZ, 128), 1) < counts[0][:, None]
    packed = jnp.concatenate([position, jnp.where(live, mass, 0.0)[None]], axis=0)
    row = jnp.stack([shift(packed, wide, PX, 1), packed, shift(packed, wide, PX, -1)])
    left = shift(row, "gy", PY, 1)
    right = shift(row, "gy", PY, -1)

    modes = exchange(modes, "gy").reshape(PY * 8, 128)
    modes = call(forward_y_kernel, (NY, 128), (modes, *t["fwd_y"]))
    modes = exchange(modes.reshape(PX, 2, 128), wide).reshape(NY, 128)
    modes = call(
        solve_x_kernel,
        (4 * PX, 128),
        (modes, *t["fwd_x"], *t["inv_x"], t["kappa_x"], t["kappa_y"], t["kappa_z"]),
    )
    fields = exchange(modes.reshape(PX, 4, 128), wide).reshape(4 * PX, 128)
    short = call(
        short_kernel,
        (3, TZ, 128),
        (listed, position, left, row, right),
        smem=1,
        scratch=[pltpu.VMEM((9, 4, TZ, 128), f32), pltpu.VMEM((3 * 128, 128), f32)],
        cost=pl.CostEstimate(
            flops=22 * TZ * NB * 128 * 128,
            bytes_accessed=400_000,
            transcendentals=2 * TZ * NB * 128 * 128,
        ),
    )
    fields = call(inverse_y_kernel, (PY, 24, 128), (fields, *t["inv_y"]))
    fields = exchange(fields, "gy")
    kicked = call(
        kick_kernel,
        (3, TZ, 128),
        (counts, fields, position, velocity, short, *t["inv_z"], t["sine_z"]),
        smem=1,
    )
    return jnp.transpose(kicked, (1, 0, 2))[None, None]


def solution(mesh):
    wide = ("gx", "gz")
    placed = (
        P(wide, "gy", None, None, None),
        P(wide, "gy", None, None),
        P(wide, "gy", None, None, None),
        P(wide, "gy", None),
        P(wide, "gy", None, None),
    )
    return jax.shard_map(
        shards,
        mesh=mesh,
        in_specs=placed,
        out_specs=P(wide, "gy", None, None, None),
        check_vma=False,
    )
```

profile of v0, /device:TPU:1, one launch (start us, length us, event | category | flops | bytes accessed | tf_op | source)
XLA Modules:
  0.0 108.0 jit_solution(8393000172992114983)
XLA Ops:
  0.0 0.0 copy-start.2
  0.0 1.6 %copy-done.2 = bf16[1024,1024]{1,0:T(8,128)(2,1)S(1)} copy-done((bf16[1024,1024]{1,0:T(8,128)(2,1)S(1)}, bf16[1024,1024]{1,0:T(8,128)(2,1)}, u32[]{:S(2)}) %copy-start.2) | copy-done | bytes 2097176
  1.6 0.0 copy-start.3
  1.6 1.6 %copy-done.3 = bf16[1024,1024]{1,0:T(8,128)(2,1)S(1)} copy-done((bf16[1024,1024]{1,0:T(8,128)(2,1)S(1)}, bf16[1024,1024]{1,0:T(8,128)(2,1)}, u32[]{:S(2)}) %copy-start.3) | copy-done | bytes 2097176
  3.2 0.0 copy-start.4
  3.2 0.7 copy-done.4
  3.9 0.0 copy-start.11
  3.9 0.7 copy-done.11
  4.6 0.0 copy-start.21
  4.6 0.7 copy-done.21
  5.3 0.0 copy-start.17
  5.3 0.0 copy-start.18
  5.3 0.0 copy-start.8
  5.3 0.0 copy-start.10
  5.3 0.0 copy-start.14
  5.3 0.0 copy-start.15
  5.3 0.0 copy-start.16
  5.3 0.0 copy-start.20
  5.3 0.0 copy-start.6
  5.4 0.0 copy-start.7
  5.4 0.0 copy-start.12
  5.4 0.0 copy-start.22
  5.4 0.0 copy-start.5
  5.4 2.3 %shard_map.199 = f32[16,8,128]{2,1,0:T(8,128)S(1)} custom-call(s32[1,16]{1,0:T(1,128)S(1)} %bitcast.39, f32[3,16,128]{2,1,0:T(8,128)S(1)} %bitcast.31, f32[16,128]{1,0:T(8,128)S(1)} %bitcast.37, bf16[1024,1024]{1,0:T(8,128)(2,1)S(1)} %copy-done.2, bf16[1024,1024]{1,0:T(8,128)(2,1)S(1)} %copy-done.3), custom_call_target="tpu_custom_call" | custom-call | tf_op jit(solution)/shard_map/pallas_call | solution.py:302
  7.7 0.0 copy-start.23
  7.7 20.8 %all_to_all.20 = f32[16,8,128]{2,1,0:T(8,128)S(1)} all-to-all(f32[16,8,128]{2,1,0:T(8,128)S(1)} %shard_map.199), channel_id=1, replica_groups=mesh['gx'=8,'gy'=16,'gz'=6] {'gy'}, dimensions={0} | all-to-all | bytes 131072 | tf_op jit(solution)/shard_map/all_to_all | solution.py:314
  28.5 0.0 copy-done.17
  28.5 0.0 copy-done.18
  28.5 0.2 shard_map.200
  28.7 24.7 %all_to_all.21 = f32[48,2,128]{2,1,0:T(2,128)S(1)} all-to-all(f32[48,2,128]{2,1,0:T(2,128)S(1)} %bitcast.35), channel_id=1, replica_groups=mesh['gx'=8,'gy'=16,'gz'=6] {'gx','gz'}, dimensions={0} | all-to-all | bytes 98304 | tf_op jit(solution)/shard_map/all_to_all | solution.py:314
  53.3 0.0 copy-done.8
  53.3 0.0 copy-done.9
  53.3 0.0 copy-done.10
  53.3 0.0 copy-done.14
  53.4 0.0 copy-done.15
  53.4 0.0 copy-done.16
  53.4 0.0 copy-done.20
  53.4 0.4 shard_map.201
  53.8 15.6 %all_to_all.22 = f32[48,4,128]{2,1,0:T(4,128)S(1)} all-to-all(f32[48,4,128]{2,1,0:T(4,128)S(1)} %bitcast.28), channel_id=1, replica_groups=mesh['gx'=8,'gy'=16,'gz'=6] {'gx','gz'}, dimensions={0} | all-to-all | bytes 196608 | tf_op jit(solution)/shard_map/all_to_all | solution.py:314
  69.4 0.0 copy-done.6
  69.4 0.0 copy-done.7
  69.4 1.2 %shard_map.202 = f32[16,24,128]{2,1,0:T(8,128)} custom-call(f32[192,128]{1,0:T(8,128)S(1)} %bitcast.29, bf16[512,48]{1,0:T(8,128)(2,1)S(1)} %copy-done.6, bf16[512,48]{1,0:T(8,128)(2,1)S(1)} %copy-done.7), custom_call_target="tpu_custom_call" | custom-call | tf_op jit(solution)/shard_map/pallas_call | solution.py:302
  70.7 6.2 %all-to-all-start.3 = ((f32[16,24,128]{2,1,0:T(8,128)}), f32[16,24,128]{2,1,0:T(8,128)S(1)}, u32[]{:S(2)}, u32[]{:S(2)}) async-start(f32[16,24,128]{2,1,0:T(8,128)} %shard_map.202), calls=%async_computation.3 | async-start | bytes 393216 | tf_op jit(solution)/shard_map/all_to_all | solution.py:314
  76.9 0.0 copy-done.12
  76.9 0.0 copy-done.22
  76.9 0.1 bitcast_select_fusion
  76.9 0.0 copy-done.5
  77.0 2.4 %collective-permute-start = (f32[4,16,128]{2,1,0:T(8,128)S(1)}, f32[4,16,128]{2,1,0:T(8,128)S(1)}, u32[]{:S(2)}, u32[]{:S(2)}) collective-permute-start(f32[4,16,128]{2,1,0:T(8,128)S(1)} %get-tuple-element.6), channel_id=1, source_target_pairs={{0,1},{1,2},{2,3},{3,4},{4,5},{5,96},{96,97},{97,98},{98,99},{99,1... | collective-permute-start | bytes 98312 | tf_op jit(solution)/shard_map/ppermute | solution.py:318
  79.4 6.2 %collective-permute-start.1 = (f32[4,16,128]{2,1,0:T(8,128)S(1)}, f32[4,16,128]{2,1,0:T(8,128)S(1)}, u32[]{:S(2)}, u32[]{:S(2)}) collective-permute-start(f32[4,16,128]{2,1,0:T(8,128)S(1)} %get-tuple-element.6), channel_id=1, source_target_pairs={{0,677},{1,0},{2,1},{3,2},{4,3},{5,4},{96,5},{97,96},{98,97},{99,9... | collective-permute-start | bytes 98312 | tf_op jit(solution)/shard_map/ppermute | solution.py:318
  85.6 0.0 collective-permute-done
  85.6 1.0 collective-permute-done.1
  86.6 2.8 %collective-permute-start.2 = (f32[3,4,16,128]{3,2,1,0:T(8,128)S(1)}, f32[3,4,16,128]{3,2,1,0:T(8,128)S(1)}, u32[]{:S(2)}, u32[]{:S(2)}) collective-permute-start(f32[3,4,16,128]{3,2,1,0:T(8,128)S(1)} %pad_maximum_fusion.mid_ref), channel_id=1, source_target_pairs={{0,6},{6,12},{12,18},{18,24},{24,30},{30,36},{36,42},{42,48},{48,5... | collective-permute-start | bytes 294920 | tf_op jit(solution)/shard_map/ppermute | solution.py:318
  89.4 0.0 collective-permute-start.3
  89.4 0.0 copy-done.23
  89.4 1.6 %collective-permute-done.2.left_ref = f32[3,4,16,128]{3,2,1,0:T(8,128)S(1)} collective-permute-done((f32[3,4,16,128]{3,2,1,0:T(8,128)S(1)}, f32[3,4,16,128]{3,2,1,0:T(8,128)S(1)}, u32[]{:S(2)}, u32[]{:S(2)}) %collective-permute-start.2) | collective-permute-done | bytes 98336 | tf_op jit(solution)/shard_map/ppermute | solution.py:318
  91.0 2.4 %collective-permute-done.3.right_ref = f32[3,4,16,128]{3,2,1,0:T(8,128)S(1)} collective-permute-done((f32[3,4,16,128]{3,2,1,0:T(8,128)S(1)}, f32[3,4,16,128]{3,2,1,0:T(8,128)S(1)}, u32[]{:S(2)}, u32[]{:S(2)}) %collective-permute-start.3) | collective-permute-done | bytes 98336 | tf_op jit(solution)/shard_map/ppermute | solution.py:318
  93.4 10.3 %shard_map.203.short_ref = f32[3,16,128]{2,1,0:T(8,128)S(1)} custom-call(s32[6,16]{1,0:T(8,128)S(1)} %bitcast.42, f32[3,16,128]{2,1,0:T(8,128)S(1)} %bitcast.33, f32[3,4,16,128]{3,2,1,0:T(8,128)S(1)} %collective-permute-done.2.left_ref, f32[3,4,16,128]{3,2,1,0:T(8,128)S(1)} %pad_maximum_fusion.mid_ref, f32[3,4,16,128]{3,2,1,0:T(8,128)S(1)} %collective-permute-done.3.right_ref), custom_call_target="tpu_custom_call" | custom-call | flops 34603008 | bytes 400000 | tf_op jit(solution)/shard_map/pallas_call | solution.py:302
  103.7 0.0 all-to-all-done.3.in_ref
  103.7 0.0 copy-done
  103.7 0.0 copy-done.13
  103.8 0.0 copy-done.19
  103.8 0.0 copy-start.1
  103.8 1.6 %copy-done.1 = bf16[1024,1024]{1,0:T(8,128)(2,1)S(1)} copy-done((bf16[1024,1024]{1,0:T(8,128)(2,1)S(1)}, bf16[1024,1024]{1,0:T(8,128)(2,1)}, u32[]{:S(2)}) %copy-start.1) | copy-done | bytes 2097176
  105.4 2.6 %shard_map.204 = f32[3,16,128]{2,1,0:T(8,128)} custom-call(s32[1,16]{1,0:T(1,128)S(1)} %bitcast.41, f32[16,24,128]{2,1,0:T(8,128)S(1)} %all-to-all-done.3.in_ref, f32[3,16,128]{2,1,0:T(8,128)S(1)} %bitcast.34, f32[3,16,128]{2,1,0:T(8,128)S(1)} %bitcast.38, f32[3,16,128]{2,1,0:T(8,128)S(1)} %shard_map.203.short_ref, bf16[1024,1024]{1,0:T(8,128)(2,1)S(1)} %copy-done, ...), custom_call_target="tpu_custom_call" | custom-call | tf_op jit(solution)/shard_map/pallas_call | solution.py:302
  (7 shorter events, 0.0 us)
Async XLA Ops:
  0.0 1.6 %copy-start.2 = (bf16[1024,1024]{1,0:T(8,128)(2,1)S(1)}, bf16[1024,1024]{1,0:T(8,128)(2,1)}, u32[]{:S(2)}) copy-start(bf16[1024,1024]{1,0:T(8,128)(2,1)} %constant.34.clone.high_ref) | copy-start | bytes 6291460
  1.6 1.6 %copy-start.3 = (bf16[1024,1024]{1,0:T(8,128)(2,1)S(1)}, bf16[1024,1024]{1,0:T(8,128)(2,1)}, u32[]{:S(2)}) copy-start(bf16[1024,1024]{1,0:T(8,128)(2,1)} %constant.35.clone.low_ref) | copy-start | bytes 6291460
  3.2 0.7 copy-start.4
  3.9 0.7 copy-start.11
  4.6 0.7 copy-start.21
  5.3 23.2 %copy-start.17 = (bf16[96,128]{1,0:T(8,128)(2,1)S(1)}, bf16[96,128]{1,0:T(8,128)(2,1)}, u32[]{:S(2)}) copy-start(bf16[96,128]{1,0:T(8,128)(2,1)} %constant.36.clone.high_ref) | copy-start | bytes 73732
  5.3 23.2 %copy-start.18 = (bf16[96,128]{1,0:T(8,128)(2,1)S(1)}, bf16[96,128]{1,0:T(8,128)(2,1)}, u32[]{:S(2)}) copy-start(bf16[96,128]{1,0:T(8,128)(2,1)} %constant.37.clone.low_ref) | copy-start | bytes 73732
  5.3 48.1 %copy-start.8 = (bf16[192,96]{1,0:T(8,128)(2,1)S(1)}, bf16[192,96]{1,0:T(8,128)(2,1)}, u32[]{:S(2)}) copy-start(bf16[192,96]{1,0:T(8,128)(2,1)} %constant.40.clone.inv_high) | copy-start | bytes 110596
  5.3 48.1 %copy-start.9 = (bf16[192,96]{1,0:T(8,128)(2,1)S(1)}, bf16[192,96]{1,0:T(8,128)(2,1)}, u32[]{:S(2)}) copy-start(bf16[192,96]{1,0:T(8,128)(2,1)} %constant.41.clone.inv_low) | copy-start | bytes 110596
  5.3 48.1 %copy-start.10 = (f32[96,1]{1,0:T(8,128)S(1)}, f32[96,1]{1,0:T(8,128)}, u32[]{:S(2)}) copy-start(f32[96,1]{1,0:T(8,128)} %constant.42.clone.kappa_x) | copy-start | bytes 1156
  5.3 48.0 %copy-start.14 = (bf16[96,96]{1,0:T(8,128)(2,1)S(1)}, bf16[96,96]{1,0:T(8,128)(2,1)}, u32[]{:S(2)}) copy-start(bf16[96,96]{1,0:T(8,128)(2,1)} %constant.38.clone.fwd_high) | copy-start | bytes 55300
  5.3 48.0 %copy-start.15 = (bf16[96,96]{1,0:T(8,128)(2,1)S(1)}, bf16[96,96]{1,0:T(8,128)(2,1)}, u32[]{:S(2)}) copy-start(bf16[96,96]{1,0:T(8,128)(2,1)} %constant.39.clone.fwd_low) | copy-start | bytes 55300
  5.3 48.0 %copy-start.16 = (f32[48,128]{1,0:T(8,128)S(1)}, f32[48,128]{1,0:T(8,128)}, u32[]{:S(2)}) copy-start(f32[48,128]{1,0:T(8,128)} %constant.43.clone.kappa_y) | copy-start | bytes 73732
  5.3 48.0 %copy-start.20 = (f32[16,128]{1,0:T(8,128)S(1)}, f32[16,128]{1,0:T(8,128)}, u32[]{:S(2)}) copy-start(f32[16,128]{1,0:T(8,128)} %constant.44.clone.kappa_z) | copy-start | bytes 24580
  5.3 64.1 %copy-start.6 = (bf16[512,48]{1,0:T(8,128)(2,1)S(1)}, bf16[512,48]{1,0:T(8,128)(2,1)}, u32[]{:S(2)}) copy-start(bf16[512,48]{1,0:T(8,128)(2,1)} %constant.45.clone.high_ref) | copy-start | bytes 147460
  5.4 64.1 %copy-start.7 = (bf16[512,48]{1,0:T(8,128)(2,1)S(1)}, bf16[512,48]{1,0:T(8,128)(2,1)}, u32[]{:S(2)}) copy-start(bf16[512,48]{1,0:T(8,128)(2,1)} %constant.46.clone.low_ref) | copy-start | bytes 147460
  5.4 71.5 %copy-start.12 = (f32[1,1,16,128]{3,2,1,0:T(8,128)S(1)}, f32[1,1,16,128]{3,2,1,0:T(8,128)}, u32[]{:S(2)}) copy-start(f32[1,1,16,128]{3,2,1,0:T(8,128)} %param.22) | copy-start | bytes 24580
  5.4 71.5 %copy-start.22 = (s32[1,1,16]{2,1,0:T(1,128)S(1)}, s32[1,1,16]{2,1,0:T(1,128)}, u32[]{:S(2)}) copy-start(s32[1,1,16]{2,1,0:T(1,128)} %param.24) | copy-start | bytes 196
  5.4 71.6 %copy-start.5 = (f32[1,1,16,3,128]{4,2,3,1,0:T(8,128)S(1)}, f32[1,1,16,3,128]{4,2,3,1,0:T(8,128)}, u32[]{:S(2)}) copy-start(f32[1,1,16,3,128]{4,2,3,1,0:T(8,128)} %param.21) | copy-start | bytes 73732
  7.7 81.6 %copy-start.23 = (s32[1,1,16,6]{2,1,3,0:T(1,128)S(1)}, s32[1,1,16,6]{2,1,3,0:T(1,128)}, u32[]{:S(2)}) copy-start(s32[1,1,16,6]{2,1,3,0:T(1,128)} %param.25) | copy-start | bytes 1156
  70.7 33.1 %all-to-all-start.3 = ((f32[16,24,128]{2,1,0:T(8,128)}), f32[16,24,128]{2,1,0:T(8,128)S(1)}, u32[]{:S(2)}, u32[]{:S(2)}) async-start(f32[16,24,128]{2,1,0:T(8,128)} %shard_map.202), calls=%async_computation.3 | async-start | bytes 393216 | tf_op jit(solution)/shard_map/all_to_all | solution.py:314
  77.0 8.6 %collective-permute-start = (f32[4,16,128]{2,1,0:T(8,128)S(1)}, f32[4,16,128]{2,1,0:T(8,128)S(1)}, u32[]{:S(2)}, u32[]{:S(2)}) collective-permute-start(f32[4,16,128]{2,1,0:T(8,128)S(1)} %get-tuple-element.6), channel_id=1, source_target_pairs={{0,1},{1,2},{2,3},{3,4},{4,5},{5,96},{96,97},{97,98},{98,99},{99,1... | collective-permute-start | bytes 98312 | tf_op jit(solution)/shard_map/ppermute | solution.py:318
  79.4 7.2 %collective-permute-start.1 = (f32[4,16,128]{2,1,0:T(8,128)S(1)}, f32[4,16,128]{2,1,0:T(8,128)S(1)}, u32[]{:S(2)}, u32[]{:S(2)}) collective-permute-start(f32[4,16,128]{2,1,0:T(8,128)S(1)} %get-tuple-element.6), channel_id=1, source_target_pairs={{0,677},{1,0},{2,1},{3,2},{4,3},{5,4},{96,5},{97,96},{98,97},{99,9... | collective-permute-start | bytes 98312 | tf_op jit(solution)/shard_map/ppermute | solution.py:318
  86.6 4.4 %collective-permute-start.2 = (f32[3,4,16,128]{3,2,1,0:T(8,128)S(1)}, f32[3,4,16,128]{3,2,1,0:T(8,128)S(1)}, u32[]{:S(2)}, u32[]{:S(2)}) collective-permute-start(f32[3,4,16,128]{3,2,1,0:T(8,128)S(1)} %pad_maximum_fusion.mid_ref), channel_id=1, source_target_pairs={{0,6},{6,12},{12,18},{18,24},{24,30},{30,36},{36,42},{42,48},{48,5... | collective-permute-start | bytes 294920 | tf_op jit(solution)/shard_map/ppermute | solution.py:318
  89.4 4.0 %collective-permute-start.3 = (f32[3,4,16,128]{3,2,1,0:T(8,128)S(1)}, f32[3,4,16,128]{3,2,1,0:T(8,128)S(1)}, u32[]{:S(2)}, u32[]{:S(2)}) collective-permute-start(f32[3,4,16,128]{3,2,1,0:T(8,128)S(1)} %pad_maximum_fusion.mid_ref), channel_id=1, source_target_pairs={{0,90},{6,0},{12,6},{18,12},{24,18},{30,24},{36,30},{42,36},{48,42... | collective-permute-start | bytes 294920 | tf_op jit(solution)/shard_map/ppermute | solution.py:318
  93.4 10.3 %copy-start = (bf16[1024,1024]{1,0:T(8,128)(2,1)S(1)}, bf16[1024,1024]{1,0:T(8,128)(2,1)}, u32[]{:S(2)}) copy-start(bf16[1024,1024]{1,0:T(8,128)(2,1)} %constant.47.clone.high_ref) | copy-start | bytes 6291460
  93.4 10.3 %copy-start.13 = (f32[1,1,16,3,128]{4,2,3,1,0:T(8,128)S(1)}, f32[1,1,16,3,128]{4,2,3,1,0:T(8,128)}, u32[]{:S(2)}) copy-start(f32[1,1,16,3,128]{4,2,3,1,0:T(8,128)} %param.23) | copy-start | bytes 73732
  93.4 10.4 %copy-start.19 = (f32[16,128]{1,0:T(8,128)S(1)}, f32[16,128]{1,0:T(8,128)}, u32[]{:S(2)}) copy-start(f32[16,128]{1,0:T(8,128)} %constant.49.clone.sine_ref) | copy-start | bytes 24580
  103.8 1.6 %copy-start.1 = (bf16[1024,1024]{1,0:T(8,128)(2,1)S(1)}, bf16[1024,1024]{1,0:T(8,128)(2,1)}, u32[]{:S(2)}) copy-start(bf16[1024,1024]{1,0:T(8,128)(2,1)} %constant.48.clone.low_ref) | copy-start | bytes 6291460
where the time goes:
time: 110 us; the launch traced here: 108 us
  blocking collectives  61 us (55%)
  starting transfers between devices  17.6 us (16%)
  Pallas kernels  17 us (15%)
  local copies, waits for them, and re-layouts  6.97 us (6%)
  waiting for transfers between devices  5.03 us (5%)
    all_to_all x3, blocking collectives, exchange(): return lax.all_to_all(value, axis, split_axis=0, concat_axis=0, tiled=True)  61 us
    pallas_call x6, Pallas kernels, call(): pl.pallas_call(kernel, out_shape=jax.ShapeDtypeStruct(shape, f32), in_spe...  17 us
    ppermute x4, starting transfers between devices, shift(): lax.ppermute(value, axis, [(i, (i + step) % count) for i in range(count)])  11.4 us
    unnamed x49, local copies, waits for them, and re-layouts  6.97 us
    all_to_all x1, starting transfers between devices, exchange(): return lax.all_to_all(value, axis, split_axis=0, concat_axis=0, tiled=True)  6.2 us
    ppermute x4, waiting for transfers between devices, shift(): lax.ppermute(value, axis, [(i, (i + step) % count) for i in range(count)])  5.03 us
  transfers between devices with their start and end apart: 5, of which 3 were waited for; matrix products, arithmetic and copies ran while one was open for 0% of the time, Pallas kernels for 10%

commit v1 on v0

v1 whole, which is shorter than its diff:
```python
import functools

import jax
import jax.numpy as jnp
import ml_dtypes
import numpy as np
from jax import lax
from jax.experimental import pallas as pl
from jax.experimental.pallas import tpu as pltpu
from jax.sharding import PartitionSpec as P

CX = 2
CY = 6
NZ = 1024
TZ = 16
NB = 6
NX = 96
NY = 96
PX = 48
PY = 16
CELLS = NZ // TZ
BLOCK = NZ // PY
HALF = BLOCK // 2
PIECES = 4 * TZ // 2

smoothing = 0.1
screening = 0.01
split_scale = 2.0
softening = 0.05
long_kick = 1.0
short_kick = 0.05

f32 = jnp.float32
bf16 = jnp.bfloat16


def halves(table):
    high = table.astype(np.float32).astype(ml_dtypes.bfloat16)
    low = (table - high.astype(np.float64)).astype(np.float32).astype(ml_dtypes.bfloat16)
    return high, low


def real_basis(length, run):
    cells = np.arange(length)[:, None]
    wave = np.arange(length // 2)
    angle = 2 * np.pi * (cells * wave[None] % length) / length
    cosine = np.cos(angle) * np.sqrt(2 / length)
    sine = np.sin(angle) * np.sqrt(2 / length)
    step = np.sin(2 * np.pi * wave / length)
    cos_slope = sine * step
    sin_slope = -cosine * step
    cosine[:, 0] = np.sqrt(1 / length)
    sine[:, 0] = np.where(cells[:, 0] % 2 == 0, 1.0, -1.0) * np.sqrt(1 / length)
    cos_slope[:, 0] = 0
    sin_slope[:, 0] = 0
    kappa_cos = 4 * np.sin(np.pi * wave / length) ** 2
    kappa_sin = kappa_cos.copy()
    kappa_sin[0] = 4.0

    def laid(first, second):
        shape = first.shape[:-1] + (-1, 1, run)
        return np.concatenate([first.reshape(shape), second.reshape(shape)], axis=-2).reshape(
            first.shape[:-1] + (length,)
        )

    return (
        laid(cosine, sine),
        laid(cos_slope, sin_slope),
        laid(kappa_cos, kappa_sin),
        laid(-step, step),
    )


def depth_basis():
    table = np.zeros((4, 2, 128, 256))
    waves = np.zeros((4, 128))
    waves[0] = np.concatenate([8 * np.arange(64), 8 * np.arange(64) + 4])
    for residue in (1, 2, 3):
        waves[residue] = 8 * np.arange(128) + residue
    angle = 2 * np.pi * (np.arange(128)[:, None] * waves[:, None] % NZ) / NZ
    cosine = np.cos(angle) * np.sqrt(2 / NZ)
    sine = np.sin(angle) * np.sqrt(2 / NZ)
    cosine[0, :, 0] = np.sqrt(1 / NZ)
    sine[0, :, 0] = np.where(np.arange(128) % 2 == 0, 1.0, -1.0) * np.sqrt(1 / NZ)
    step = np.sin(2 * np.pi * waves / NZ)
    kappa_cos = 4 * np.sin(np.pi * waves / NZ) ** 2
    kappa_sin = kappa_cos.copy()
    step[0, 0] = 0
    kappa_sin[0, 0] = 4.0

    def laid(first, second):
        shape = first.shape[:-1] + (4, 1, HALF)
        return np.concatenate([first.reshape(shape), second.reshape(shape)], axis=-2).reshape(
            first.shape[:-1] + (256,)
        )

    table[:, 0] = laid(cosine, sine)
    table[:, 1] = laid(-sine, cosine)
    table[0, 1, :, 128:] = table[0, 0, :, 128:]
    table[0, 0, :, 128:] = 0
    table[0, 1, :, :128] = 0
    return (
        table.reshape(4, 256, 256),
        laid(kappa_cos, kappa_sin).reshape(NZ),
        laid(-step, step).reshape(NZ),
    )


ROOT_HALF = float(np.sqrt(0.5))


def waves_of(cells):
    total = [cells[a] + cells[a + 4] for a in range(4)]
    apart = [cells[a] - cells[a + 4] for a in range(4)]
    even, odd = total[0] + total[2], total[1] + total[3]
    less, more = (apart[1] - apart[3]) * ROOT_HALF, (apart[1] + apart[3]) * ROOT_HALF
    pairs = (
        (even + odd, even - odd),
        (apart[0] + less, more + apart[2]),
        (total[0] - total[2], total[1] - total[3]),
        (apart[0] - less, more - apart[2]),
    )
    return [jnp.concatenate(pair, axis=1) for pair in pairs]


def cells_of(pairs):
    (zero, four), one, two, three = [(pair[:, :128], pair[:, 128:]) for pair in pairs]
    plus, minus = zero + four, zero - four
    even = (plus + two[0], minus + two[1], plus - two[0], minus - two[1])
    less, more = (one[0] - three[0]) * ROOT_HALF, (one[1] + three[1]) * ROOT_HALF
    odd = (one[0] + three[0], more + less, one[1] - three[1], more - less)
    return [even[a] + odd[a] for a in range(4)] + [even[a] - odd[a] for a in range(4)]


@functools.lru_cache(None)
def tables():
    table_z, kappa_z, sine_z = depth_basis()
    basis_x, slope_x, kappa_x, _ = real_basis(NX, 1)
    basis_y, slope_y, kappa_y, _ = real_basis(NY, 1)
    out = {}
    out["fwd_z"] = np.concatenate(halves(table_z), axis=0)
    out["inv_z"] = np.concatenate(halves(table_z.transpose(0, 2, 1)), axis=0)
    pad_y = np.zeros((2, PX, PY, 8))
    pad_y[..., :CY] = basis_y.T.reshape(PX, 2, PY, CY).transpose(1, 0, 2, 3)
    out["fwd_y"] = halves(pad_y.reshape(NY, PY * 8))
    out["fwd_x"] = halves(basis_x.reshape(PX, CX, NX).transpose(2, 1, 0).reshape(NX, CX * PX))
    both = np.stack([slope_x.reshape(PX, CX, NX), basis_x.reshape(PX, CX, NX)])
    out["inv_x"] = halves(both.transpose(0, 2, 1, 3).reshape(2 * CX * PX, NX))

    rows = np.zeros((2, PY, 3, CY, 2, PX))
    spread = [table.reshape(PY, CY, PX, 2).transpose(3, 0, 1, 2) for table in (basis_y, slope_y)]
    rows[:, :, 0, :, 0] = spread[0]
    rows[:, :, 1, :, 1] = spread[1]
    rows[:, :, 2, :, 1] = spread[0]
    out["inv_y"] = halves(rows.reshape(2 * PY * 3 * CY, 2 * PX))
    out["kappa_x"] = kappa_x[:, None].astype(np.float32)
    out["kappa_y"] = np.repeat(kappa_y.reshape(PX, 2), BLOCK, axis=1).astype(np.float32)
    out["kappa_z"] = np.tile(kappa_z.reshape(PY, BLOCK), (1, 2)).astype(np.float32)
    out["sine_z"] = np.tile(sine_z.reshape(PY, BLOCK), (1, 2)).astype(np.float32)
    return out


def split(value):
    high = value.astype(bf16)
    return high, (value - high.astype(f32)).astype(bf16)


def dot(left, right):
    return lax.dot_general(left, right, (((1,), (0,)), ((), ())), preferred_element_type=f32)


def dot_t(left, right):
    return lax.dot_general(left, right, (((1,), (1,)), ((), ())), preferred_element_type=f32)


def table_dot(high_ref, low_ref, value):
    high, low = split(value)
    return dot(high_ref[...], high) + dot(high_ref[...], low) + dot(low_ref[...], high)


def dot_table(value, table_ref, at):
    rows = value.shape[0]
    high, low = split(value)
    both = dot(jnp.concatenate([high, low], axis=0), table_ref[at])
    return both[:rows] + both[rows:] + dot(high, table_ref[4 + at])


def iota(shape, dim):
    return lax.broadcasted_iota(jnp.int32, shape, dim)


def plane_weights(pos_ref, tile):
    row = iota((16, 128), 0)
    row_x = (row >> 3).astype(f32)
    row_y = (row & 7).astype(f32)
    x = jnp.clip(pos_ref[0, tile : tile + 1, :] * CX - 0.5, 0.0, 1.0)
    y = jnp.clip(pos_ref[1, tile : tile + 1, :] * CY - 0.5, 0.0, CY - 1.0)
    return (1.0 - jnp.abs(x - row_x)) * jnp.maximum(1.0 - jnp.abs(y - row_y), 0.0)


def depth_weights(pos_ref, tile):
    z = (tile + pos_ref[2, tile : tile + 1, :]) * CELLS - 0.5 - (tile * CELLS - CELLS // 2)
    return jnp.maximum(1.0 - jnp.abs(z - iota((128, 128), 0).astype(f32)), 0.0)


def deposit_kernel(
    counts_hbm,
    pos_hbm,
    mass_hbm,
    table_hbm,
    out_ref,
    packed_ref,
    live_ref,
    counts,
    pos_ref,
    mass_ref,
    table_ref,
    arrived,
):
    loads = [
        pltpu.make_async_copy(source, held, arrived.at[at])
        for at, (source, held) in enumerate(
            (
                (counts_hbm, counts),
                (pos_hbm, pos_ref),
                (mass_hbm, mass_ref),
                (table_hbm, table_ref),
            )
        )
    ]
    for load in loads:
        load.start()
    for load in loads[:3]:
        load.wait()
    packed_ref[:3] = pos_ref[...]
    slot = iota((1, 128), 1)
    windows = []
    for tile in range(TZ):
        live = slot < counts[0, tile]
        live_ref[tile : tile + 1, :] = jnp.where(live, 1.0, 0.0)
        mass = jnp.where(live, mass_ref[tile : tile + 1, :], 0.0)
        packed_ref[3, tile : tile + 1, :] = mass
        flat_high, flat_low = split(plane_weights(pos_ref, tile) * mass)
        deep_high, deep_low = split(depth_weights(pos_ref, tile))
        windows.append(
            dot_t(flat_high, deep_high) + dot_t(flat_high, deep_low) + dot_t(flat_low, deep_high)
        )
    even = jnp.concatenate(windows[0::2], axis=1)
    odd = jnp.concatenate(windows[1::2], axis=1)
    density = pltpu.roll(even, NZ - CELLS // 2, 1) + pltpu.roll(odd, CELLS // 2, 1)
    pairs = waves_of([density[:, 128 * a : 128 * a + 128] for a in range(8)])
    loads[3].wait()
    modes = [dot_table(value, table_ref, at) for at, value in enumerate(pairs)]
    first = iota((8, 128), 1) < BLOCK
    for pair in range(PY // 2):
        part = modes[pair // 2][:, 128 * (pair % 2) : 128 * (pair % 2) + 128]
        near = part[:8]
        far = part[8:]
        out_ref[2 * pair] = jnp.where(first, near, pltpu.roll(far, BLOCK, 1))
        out_ref[2 * pair + 1] = jnp.where(first, pltpu.roll(near, BLOCK, 1), far)


def forward_y_kernel(in_ref, high_ref, low_ref, packed_ref, out_ref):
    value = table_dot(high_ref, low_ref, in_ref[...])
    for at in range(2):
        out_ref[pl.ds(at, PX, stride=4), :] = value[PX * at : PX * (at + 1)]
        out_ref[pl.ds(2 + at, PIECES, stride=4), :] = packed_ref[pl.ds(at, PIECES, stride=2), :]
        out_ref[pl.ds(4 * PIECES + 2 + at, PX - PIECES, stride=4), :] = jnp.zeros(
            (PX - PIECES, 128), f32
        )


def solve_x_kernel(
    in_ref, fwd_high, fwd_low, inv_high, inv_low, kappa_x, kappa_y, kappa_z, out_ref
):
    at_x = lax.axis_index(("gx", "gz"))
    at_y = lax.axis_index("gy")
    first = iota((PX, 128), 1) < BLOCK
    wave_a = in_ref[pl.ds(0, PX, stride=4), :]
    wave_b = in_ref[pl.ds(1, PX, stride=4), :]
    cells_0 = jnp.where(first, wave_a, pltpu.roll(wave_b, BLOCK, 1))
    cells_1 = jnp.where(first, pltpu.roll(wave_a, BLOCK, 1), wave_b)
    spectrum = table_dot(fwd_high, fwd_low, jnp.concatenate([cells_0, cells_1], axis=0))
    kappa_sum = kappa_x[...] + (kappa_y[pl.ds(at_x, 1), :] + kappa_z[pl.ds(at_y, 1), :])
    potential = spectrum * (-jnp.exp(-smoothing * kappa_sum) / (kappa_sum + screening))
    fields = table_dot(inv_high, inv_low, potential)
    for at in range(4):
        out_ref[pl.ds(at, PX, stride=8), :] = fields[PX * at : PX * (at + 1)]
    for at in range(2):
        piece = in_ref[pl.ds(2 + at, PX, stride=4), :]
        out_ref[pl.ds(4 + at, PX, stride=8), :] = pltpu.roll(piece, 1, 0)
        out_ref[pl.ds(6 + at, PX, stride=8), :] = pltpu.roll(piece, PX - 1, 0)


def inverse_y_kernel(in_ref, high_ref, low_ref, packed_ref, out_ref, row_ref):
    rows = PY * 3 * CY
    first = iota((rows, 128), 1) < BLOCK
    cells = [
        jnp.concatenate([in_ref[pl.ds(at, PX, stride=8), :] for at in (x, x + 2)], axis=0)
        for x in range(CX)
    ]
    value = table_dot(high_ref, low_ref, jnp.concatenate(cells, axis=1))
    cos_0, cos_1 = value[:rows, :128], value[:rows, 128:]
    sin_0, sin_1 = value[rows:, :128], value[rows:, 128:]
    cell_0 = cos_0 + pltpu.roll(sin_0, BLOCK, 1)
    cell_1 = pltpu.roll(cos_1, BLOCK, 1) + sin_1
    out_ref[...] = jnp.where(first, cell_0, cell_1)
    row_ref[1] = packed_ref[...]
    for at in range(2):
        for side in range(2):
            row_ref[2 * side, pl.ds(at, PIECES, stride=2), :] = in_ref[
                pl.ds(4 + 2 * side + at, PIECES, stride=8), :
            ]


def kick_kernel(
    live_ref, in_ref, pos_ref, vel_ref, short_ref, table_ref, sine_ref, out_ref
):
    first = iota((24, 128), 1) < BLOCK
    cosines = (iota((8, 128), 1) & (BLOCK - 1)) < HALF

    def block(at):
        last = PY * 3 * CY - 8
        parts = []
        for row in range(3 * CY * at, 3 * CY * (at + 1), CY):
            part = in_ref[min(row, last) : min(row, last) + 8, :]
            parts.append(part if row <= last else pltpu.roll(part, 8 - (row - last), 0))
        turned = jnp.where(
            cosines, pltpu.roll(parts[2], 128 - HALF, 1), pltpu.roll(parts[2], HALF, 1)
        )
        return jnp.concatenate(parts[:2] + [turned * sine_ref[at : at + 1, :]], axis=0)

    near, far = [], []
    for pair in range(PY // 2):
        a, b = block(2 * pair), block(2 * pair + 1)
        near.append(jnp.where(first, a, pltpu.roll(b, BLOCK, 1)))
        far.append(jnp.where(first, pltpu.roll(a, BLOCK, 1), b))
    modes = [jnp.concatenate(parts, axis=0) for parts in zip(near, far)]
    pairs = [
        dot_table(jnp.concatenate(modes[2 * at : 2 * at + 2], axis=1), table_ref, at)
        for at in range(4)
    ]
    forces = jnp.concatenate(cells_of(pairs), axis=1)
    shifted = (
        pltpu.roll(forces, CELLS // 2, 1),
        pltpu.roll(forces, NZ - CELLS // 2, 1),
    )
    for tile in range(TZ):
        start = 128 * (tile // 2)
        window = shifted[tile % 2][:, start : start + 128]
        high, low = split(window)
        deep_high, deep_low = split(depth_weights(pos_ref, tile))
        both = dot(jnp.concatenate([high, low], axis=0), deep_high)
        picked = both[:48] + both[48:] + dot(high, deep_low)
        flat = plane_weights(pos_ref, tile)
        live = live_ref[tile : tile + 1, :]
        for comp in range(3):
            at = 8 * comp
            total = flat[:8] * picked[at : at + 8] + flat[8:] * picked[24 + at : 32 + at]
            long_accel = jnp.sum(total, axis=0, keepdims=True)
            kick = long_kick * long_accel + short_kick * short_ref[comp, tile : tile + 1, :]
            out_ref[comp, tile : tile + 1, :] = vel_ref[comp, tile : tile + 1, :] + live * kick


def short_kernel(listed, left_ref, mid_ref, right_ref, out_ref, shell, sums_even, sums_odd):
    for at, ref in enumerate((left_ref, mid_ref, right_ref)):
        for dx in range(3):
            shell[3 * dx + at] = ref[dx]

    def pairs(tile, sums):
        rows = [shell[4, comp, pl.ds(tile, 1), :] for comp in range(3)]
        columns = jnp.concatenate(rows + [jnp.zeros((5, 128), f32)], axis=0).T
        sources = []
        for entry in range(NB):
            code = listed[entry, tile]
            group = code >> 4
            layer = code & (TZ - 1)
            step_x = (group * 11) >> 5
            step_y = group - 3 * step_x
            step_z = (layer - tile + 1) & (TZ - 1)
            shifts = [(step - 1).astype(f32) for step in (step_x, step_y, step_z)]
            source = [shell[group, comp, pl.ds(layer, 1), :] for comp in range(4)]
            sources.append([source[comp] + shifts[comp] for comp in range(3)] + [source[3]])
        for chunk in range(16):
            part = slice(8 * chunk, 8 * chunk + 8)
            own = [jnp.broadcast_to(columns[part, comp : comp + 1], (8, 128)) for comp in range(3)]
            totals = [None] * 3
            for x, y, z, mass in sources:
                apart = [x - own[0], y - own[1], z - own[2]]
                square = apart[0] * apart[0] + apart[1] * apart[1] + apart[2] * apart[2]
                root = lax.rsqrt(square + softening)
                strength = (mass * jnp.exp(square * (-1.0 / split_scale))) * (root * root * root)
                for comp in range(3):
                    term = strength * apart[comp]
                    totals[comp] = term if totals[comp] is None else totals[comp] + term
            for comp in range(3):
                sums[128 * comp + 8 * chunk : 128 * comp + 8 * chunk + 8, :] = totals[comp]

    def add_up(tile, sums):
        ones = jnp.ones((8, 128), bf16)
        high, low = split(sums[...])
        total = dot_t(ones, high) + dot_t(ones, low)
        for comp in range(3):
            out_ref[comp, pl.ds(tile, 1), :] = total[:1, 128 * comp : 128 * comp + 128]

    def two(at, carry):
        add_up(2 * at, sums_even)
        pairs(2 * at + 1, sums_odd)
        add_up(2 * at + 1, sums_odd)
        pairs(2 * at + 2, sums_even)
        return carry

    pairs(0, sums_even)
    lax.fori_loop(0, TZ // 2 - 1, two, 0)
    add_up(TZ - 2, sums_even)
    pairs(TZ - 1, sums_odd)
    add_up(TZ - 1, sums_odd)


def call(kernel, shapes, operands, spaces="", scratch=(), cost=None, room=24 << 20):
    space_of = {"s": pltpu.SMEM, "h": pltpu.HBM, "a": pl.ANY, "v": pltpu.VMEM}
    spaces = spaces.ljust(len(operands), "v")
    return pl.pallas_call(
        kernel,
        out_shape=[jax.ShapeDtypeStruct(shape, f32) for shape in shapes],
        in_specs=[pl.BlockSpec(memory_space=space_of[space]) for space in spaces],
        out_specs=[pl.BlockSpec(memory_space=pltpu.VMEM)] * len(shapes),
        scratch_shapes=scratch,
        cost_estimate=cost,
        compiler_params=pltpu.CompilerParams(vmem_limit_bytes=room),
    )(*operands)


def exchange(value, axis):
    return lax.all_to_all(value, axis, split_axis=0, concat_axis=0, tiled=True)


def shift(value, axis, count, step):
    return lax.ppermute(value, axis, [(i, (i + step) % count) for i in range(count)])


def short_range(*operands):
    pairs = TZ * NB * 128 * 128
    (short,) = call(
        short_kernel,
        [(3, TZ, 128)],
        operands,
        spaces="s",
        scratch=[pltpu.VMEM((9, 4, TZ, 128), f32)] + [pltpu.VMEM((3 * 128, 128), f32)] * 2,
        cost=pl.CostEstimate(flops=40_000 * pairs, bytes_accessed=400_000, transcendentals=2 * pairs),
    )
    return short


def shards(positions, masses, velocities, tile_counts, neighbour_list):
    t = tables()
    wide = ("gx", "gz")
    position = jnp.transpose(positions[0, 0], (1, 0, 2))
    velocity = jnp.transpose(velocities[0, 0], (1, 0, 2))
    mass = masses[0, 0]
    counts = tile_counts[0]
    listed = jnp.transpose(neighbour_list[0, 0], (1, 0))

    tile_shape = (4, TZ, 128)
    modes, packed, live = call(
        deposit_kernel,
        [(PY, 8, 128), tile_shape, (TZ, 128)],
        (counts, position, mass, t["fwd_z"]),
        spaces="hhhh",
        scratch=[
            pltpu.SMEM((1, TZ), jnp.int32),
            pltpu.VMEM((3, TZ, 128), f32),
            pltpu.VMEM((TZ, 128), f32),
            pltpu.VMEM((8, 256, 256), bf16),
            pltpu.SemaphoreType.DMA((4,)),
        ],
        room=63_400_000,
    )
    modes = exchange(modes, "gy").reshape(PY * 8, 128)
    packed = packed.reshape(4 * TZ, 128)
    (modes,) = call(forward_y_kernel, [(4 * PX, 128)], (modes, *t["fwd_y"], packed))
    modes = exchange(modes.reshape(PX, 4, 128), wide).reshape(4 * PX, 128)
    waves = (t["kappa_x"], t["kappa_y"], t["kappa_z"])
    (fields,) = call(
        solve_x_kernel, [(8 * PX, 128)], (modes, *t["fwd_x"], *t["inv_x"], *waves)
    )
    fields = exchange(fields.reshape(PX, 8, 128), wide).reshape(8 * PX, 128)
    fields, row = call(
        inverse_y_kernel,
        [(PY * 3 * CY, 128), (3, 4 * TZ, 128)],
        (fields, *t["inv_y"], packed),
    )
    row = row.reshape(3, 4, TZ, 128)
    left = shift(row, "gy", PY, 1)
    right = shift(row, "gy", PY, -1)
    fields = exchange(fields.reshape(PY, 3 * CY // 2, 2, 128), "gy").reshape(PY * 3 * CY, 128)
    short = short_range(listed, left, row, right)
    (kicked,) = call(
        kick_kernel,
        [(3, TZ, 128)],
        (live, fields, position, velocity, short, t["inv_z"], t["sine_z"]),
    )
    return jnp.transpose(kicked, (1, 0, 2))[None, None]


def solution(mesh):
    wide = ("gx", "gz")
    placed = (
        P(wide, "gy", None, None, None),
        P(wide, "gy", None, None),
        P(wide, "gy", None, None, None),
        P(wide, "gy", None),
        P(wide, "gy", None, None),
    )
    return jax.shard_map(
        shards,
        mesh=mesh,
        in_specs=placed,
        out_specs=P(wide, "gy", None, None, None),
        check_vma=False,
    )
```

time: 110 us -> 90.5 us (0.82); the launches traced: 108 us -> 90.1 us
  starting transfers between devices: 17.6 us -> 9.89 us
  local copies, waits for them, and re-layouts: 6.97 us -> 0.12 us
  Pallas kernels: 17 us -> 13.5 us
  blocking collectives: 61 us -> 64.3 us
  waiting for transfers between devices: 5.03 us -> 2 us
    ppermute x4 -> x2, starting transfers between devices: 11.4 us -> 3.68 us  [shift(): lax.ppermute(value, axis, [(i, (i + step) % count) for i in range(count)])]
    unnamed x49 -> x37, local copies, waits for them, and re-layouts: 6.97 us -> 0.12 us
    ppermute x4 -> x2, waiting for transfers between devices: 5.03 us -> 0.01 us  [shift(): lax.ppermute(value, axis, [(i, (i + step) % count) for i in range(count)])]
    pallas_call x6, Pallas kernels: 17 us -> 13.5 us  [call(): pl.pallas_call(kernel, out_shape=[jax.ShapeDtypeStruct(shape, f32) for sh...]
    all_to_all x3, blocking collectives: 61 us -> 64.3 us  [exchange(): return lax.all_to_all(value, axis, split_axis=0, concat_axis=0, tiled=True)]
    all_to_all x1, waiting for transfers between devices: 0.01 us -> 2 us  [exchange(): return lax.all_to_all(value, axis, split_axis=0, concat_axis=0, tiled=True)]
  transfers between devices with their start and end apart: 5 -> 3, of which waited for: 3 -> 1; matrix products, arithmetic and copies ran while one was open for 0% -> 0% of each run, Pallas kernels for 10% -> 8%
where the time goes in v1:
time: 90.5 us; the launch traced here: 90.1 us
  blocking collectives  64.3 us (71%)
  Pallas kernels  13.5 us (15%)
  starting transfers between devices  9.89 us (11%)
  waiting for transfers between devices  2 us (2%)
    all_to_all x3, blocking collectives, exchange(): return lax.all_to_all(value, axis, split_axis=0, concat_axis=0, tiled=True)  64.3 us
    pallas_call x6, Pallas kernels, call(): pl.pallas_call(kernel, out_shape=[jax.ShapeDtypeStruct(shape, f32) for sh...  13.5 us
    all_to_all x1, starting transfers between devices, exchange(): return lax.all_to_all(value, axis, split_axis=0, concat_axis=0, tiled=True)  6.21 us
    ppermute x2, starting transfers between devices, shift(): lax.ppermute(value, axis, [(i, (i + step) % count) for i in range(count)])  3.68 us
    all_to_all x1, waiting for transfers between devices, exchange(): return lax.all_to_all(value, axis, split_axis=0, concat_axis=0, tiled=True)  2 us
  transfers between devices with their start and end apart: 3, of which 1 were waited for; matrix products, arithmetic and copies ran while one was open for 0% of the time, Pallas kernels for 8%

profile of v1, /device:TPU:1, one launch (start us, length us, event | category | flops | bytes accessed | tf_op | source)
XLA Modules:
  0.0 90.1 jit_solution(17028004308041948569)
XLA Ops:
  0.0 2.8 %shard_map.181 = (f32[16,8,128]{2,1,0:T(8,128)}, f32[4,16,128]{2,1,0:T(8,128)}, f32[16,128]{1,0:T(8,128)}) custom-call(s32[1,16]{1,0:T(1,128)} %bitcast.41, f32[3,16,128]{2,1,0:T(8,128)} %bitcast.33, f32[16,128]{1,0:T(8,128)} %bitcast.40, bf16[8,256,256]{2,1,0:T(8,128)(2,1)} %constant.28.clone.table_hbm), custom_call_target="tpu_custom_call" | custom-call | tf_op jit(solution)/shard_map/pallas_call | solution.py:423
  2.8 0.0 copy-start.3
  2.8 0.0 copy-start.12
  2.8 0.0 copy-start.13
  2.8 21.8 %all_to_all.20 = f32[16,8,128]{2,1,0:T(8,128)S(1)} all-to-all(f32[16,8,128]{2,1,0:T(8,128)} %get-tuple-element.11), channel_id=1, replica_groups=mesh['gx'=8,'gy'=16,'gz'=6] {'gy'}, dimensions={0} | all-to-all | bytes 131072 | tf_op jit(solution)/shard_map/all_to_all | solution.py:435
  24.6 0.0 copy-done.3
  24.6 0.0 copy-done.12
  24.6 0.0 copy-done.13
  24.6 0.0 copy-start.10
  24.6 0.0 copy-start.16
  24.6 0.2 shard_map.182
  24.8 0.0 copy-start.5
  24.8 0.0 copy-start.6
  24.8 0.0 copy-start.7
  24.8 0.0 copy-start.8
  24.8 0.0 copy-start.9
  24.8 24.9 %all_to_all.21 = f32[48,4,128]{2,1,0:T(4,128)S(1)} all-to-all(f32[48,4,128]{2,1,0:T(4,128)S(1)} %bitcast.29), channel_id=1, replica_groups=mesh['gx'=8,'gy'=16,'gz'=6] {'gx','gz'}, dimensions={0} | all-to-all | bytes 196608 | tf_op jit(solution)/shard_map/all_to_all | solution.py:435
  49.7 0.0 copy-done.10
  49.7 0.0 copy-done.16
  49.7 0.0 copy-done.5
  49.7 0.0 copy-done.6
  49.7 0.0 copy-done.7
  49.7 0.0 copy-done.8
  49.7 0.0 copy-done.9
  49.7 0.4 shard_map.183
  50.2 0.0 copy-start.1
  50.2 0.0 copy-start.2
  50.2 17.7 %all_to_all.22 = f32[48,8,128]{2,1,0:T(8,128)S(1)} all-to-all(f32[48,8,128]{2,1,0:T(8,128)S(1)} %bitcast.25), channel_id=1, replica_groups=mesh['gx'=8,'gy'=16,'gz'=6] {'gx','gz'}, dimensions={0} | all-to-all | bytes 393216 | tf_op jit(solution)/shard_map/all_to_all | solution.py:435
  67.9 0.0 copy-done.1
  67.9 0.0 copy-done.2
  67.9 1.1 %shard_map.184 = (f32[288,128]{1,0:T(8,128)}, f32[3,64,128]{2,1,0:T(8,128)S(1)}) custom-call(f32[384,128]{1,0:T(8,128)S(1)} %bitcast.26, bf16[576,96]{1,0:T(8,128)(2,1)S(1)} %copy-done.1, bf16[576,96]{1,0:T(8,128)(2,1)S(1)} %copy-done.2, f32[64,128]{1,0:T(8,128)S(1)} %bitcast.32), custom_call_target="tpu_custom_call" | custom-call | tf_op jit(solution)/shard_map/pallas_call | solution.py:423
  69.0 0.0 copy-start.17
  69.0 3.7 %collective-permute-start = (f32[3,4,16,128]{3,2,1,0:T(8,128)S(1)}, f32[3,4,16,128]{3,2,1,0:T(8,128)S(1)}, u32[]{:S(2)}, u32[]{:S(2)}) collective-permute-start(f32[3,4,16,128]{3,2,1,0:T(8,128)S(1)} %bitcast.37), channel_id=1, source_target_pairs={{0,6},{6,12},{12,18},{18,24},{24,30},{30,36},{36,42},{42,48},{48,5... | collective-permute-start | bytes 294920 | tf_op jit(solution)/shard_map/ppermute | solution.py:439
  72.7 0.0 collective-permute-start.1
  72.7 0.0 copy-done.17
  72.7 6.2 %all-to-all-start.3 = ((f32[16,9,2,128]{3,2,1,0:T(2,128)}), f32[16,9,2,128]{3,2,1,0:T(2,128)S(1)}, u32[]{:S(2)}, u32[]{:S(2)}) async-start(f32[16,9,2,128]{3,2,1,0:T(2,128)} %bitcast.10), calls=%async_computation.3 | async-start | bytes 294912 | tf_op jit(solution)/shard_map/all_to_all | solution.py:435
  78.9 0.0 collective-permute-done.left_ref
  78.9 0.0 collective-permute-done.1.right_ref
  78.9 0.0 copy-start
  78.9 0.0 copy-start.4
  78.9 0.0 copy-start.11
  79.0 0.0 copy-start.14
  79.0 0.0 copy-start.15
  79.0 7.5 %shard_map.185.short_ref = f32[3,16,128]{2,1,0:T(8,128)S(1)} custom-call(s32[6,16]{1,0:T(8,128)S(1)} %bitcast.36, f32[3,4,16,128]{3,2,1,0:T(8,128)S(1)} %collective-permute-done.left_ref, f32[3,4,16,128]{3,2,1,0:T(8,128)S(1)} %bitcast.39, f32[3,4,16,128]{3,2,1,0:T(8,128)S(1)} %collective-permute-done.1.right_ref), custom_call_target="tpu_custom_call" | custom-call | flops 62914560000 | bytes 400000 | tf_op jit(solution)/shard_map/pallas_call | solution.py:423
  86.5 2.0 %all-to-all-done.3 = f32[16,9,2,128]{3,2,1,0:T(2,128)S(1)} async-done(((f32[16,9,2,128]{3,2,1,0:T(2,128)}), f32[16,9,2,128]{3,2,1,0:T(2,128)S(1)}, u32[]{:S(2)}, u32[]{:S(2)}) %all-to-all-start.3) | async-done | bytes 147488 | tf_op jit(solution)/shard_map/all_to_all | solution.py:435
  88.5 0.0 copy-done
  88.5 0.0 copy-done.4
  88.5 0.0 copy-done.11
  88.5 0.0 copy-done.14
  88.5 0.0 copy-done.15
  88.5 1.6 %shard_map.186 = f32[3,16,128]{2,1,0:T(8,128)} custom-call(f32[16,128]{1,0:T(8,128)S(1)} %copy-done.15, f32[288,128]{1,0:T(8,128)S(1)} %bitcast.27, f32[3,16,128]{2,1,0:T(8,128)S(1)} %bitcast.34, f32[3,16,128]{2,1,0:T(8,128)S(1)} %bitcast.35, f32[3,16,128]{2,1,0:T(8,128)S(1)} %shard_map.185.short_ref, bf16[8,256,256]{2,1,0:T(8,128)(2,1)S(1)} %copy-done, ...), custom_call_target="tpu_custom_call" | custom-call | tf_op jit(solution)/shard_map/pallas_call | solution.py:423
  (1 shorter events, 0.0 us)
Async XLA Ops:
  2.8 21.8 %copy-start.3 = (f32[4,16,128]{2,1,0:T(8,128)S(1)}, f32[4,16,128]{2,1,0:T(8,128)}, u32[]{:S(2)}) copy-start(f32[4,16,128]{2,1,0:T(8,128)} %get-tuple-element.12) | copy-start | bytes 98308
  2.8 21.8 %copy-start.12 = (bf16[96,128]{1,0:T(8,128)(2,1)S(1)}, bf16[96,128]{1,0:T(8,128)(2,1)}, u32[]{:S(2)}) copy-start(bf16[96,128]{1,0:T(8,128)(2,1)} %constant.29.clone.high_ref) | copy-start | bytes 73732
  2.8 21.8 %copy-start.13 = (bf16[96,128]{1,0:T(8,128)(2,1)S(1)}, bf16[96,128]{1,0:T(8,128)(2,1)}, u32[]{:S(2)}) copy-start(bf16[96,128]{1,0:T(8,128)(2,1)} %constant.30.clone.low_ref) | copy-start | bytes 73732
  24.6 25.1 %copy-start.10 = (f32[48,128]{1,0:T(8,128)S(1)}, f32[48,128]{1,0:T(8,128)}, u32[]{:S(2)}) copy-start(f32[48,128]{1,0:T(8,128)} %constant.36.clone.kappa_y) | copy-start | bytes 73732
  24.6 25.1 %copy-start.16 = (f32[16,128]{1,0:T(8,128)S(1)}, f32[16,128]{1,0:T(8,128)}, u32[]{:S(2)}) copy-start(f32[16,128]{1,0:T(8,128)} %constant.37.clone.kappa_z) | copy-start | bytes 24580
  24.8 24.9 %copy-start.5 = (bf16[192,96]{1,0:T(8,128)(2,1)S(1)}, bf16[192,96]{1,0:T(8,128)(2,1)}, u32[]{:S(2)}) copy-start(bf16[192,96]{1,0:T(8,128)(2,1)} %constant.33.clone.inv_high) | copy-start | bytes 110596
  24.8 24.9 %copy-start.6 = (bf16[192,96]{1,0:T(8,128)(2,1)S(1)}, bf16[192,96]{1,0:T(8,128)(2,1)}, u32[]{:S(2)}) copy-start(bf16[192,96]{1,0:T(8,128)(2,1)} %constant.34.clone.inv_low) | copy-start | bytes 110596
  24.8 24.9 %copy-start.7 = (f32[96,1]{1,0:T(8,128)S(1)}, f32[96,1]{1,0:T(8,128)}, u32[]{:S(2)}) copy-start(f32[96,1]{1,0:T(8,128)} %constant.35.clone.kappa_x) | copy-start | bytes 1156
  24.8 24.9 %copy-start.8 = (bf16[96,96]{1,0:T(8,128)(2,1)S(1)}, bf16[96,96]{1,0:T(8,128)(2,1)}, u32[]{:S(2)}) copy-start(bf16[96,96]{1,0:T(8,128)(2,1)} %constant.31.clone.fwd_high) | copy-start | bytes 55300
  24.8 24.9 %copy-start.9 = (bf16[96,96]{1,0:T(8,128)(2,1)S(1)}, bf16[96,96]{1,0:T(8,128)(2,1)}, u32[]{:S(2)}) copy-start(bf16[96,96]{1,0:T(8,128)(2,1)} %constant.32.clone.fwd_low) | copy-start | bytes 55300
  50.2 17.7 %copy-start.1 = (bf16[576,96]{1,0:T(8,128)(2,1)S(1)}, bf16[576,96]{1,0:T(8,128)(2,1)}, u32[]{:S(2)}) copy-start(bf16[576,96]{1,0:T(8,128)(2,1)} %constant.38.clone.high_ref) | copy-start | bytes 331780
  50.2 17.7 %copy-start.2 = (bf16[576,96]{1,0:T(8,128)(2,1)S(1)}, bf16[576,96]{1,0:T(8,128)(2,1)}, u32[]{:S(2)}) copy-start(bf16[576,96]{1,0:T(8,128)(2,1)} %constant.39.clone.low_ref) | copy-start | bytes 331780
  69.0 3.7 %copy-start.17 = (s32[1,1,16,6]{2,1,3,0:T(1,128)S(1)}, s32[1,1,16,6]{2,1,3,0:T(1,128)}, u32[]{:S(2)}) copy-start(s32[1,1,16,6]{2,1,3,0:T(1,128)} %param.23) | copy-start | bytes 1156
  69.0 9.9 %collective-permute-start = (f32[3,4,16,128]{3,2,1,0:T(8,128)S(1)}, f32[3,4,16,128]{3,2,1,0:T(8,128)S(1)}, u32[]{:S(2)}, u32[]{:S(2)}) collective-permute-start(f32[3,4,16,128]{3,2,1,0:T(8,128)S(1)} %bitcast.37), channel_id=1, source_target_pairs={{0,6},{6,12},{12,18},{18,24},{24,30},{30,36},{36,42},{42,48},{48,5... | collective-permute-start | bytes 294920 | tf_op jit(solution)/shard_map/ppermute | solution.py:439
  72.7 6.2 %collective-permute-start.1 = (f32[3,4,16,128]{3,2,1,0:T(8,128)S(1)}, f32[3,4,16,128]{3,2,1,0:T(8,128)S(1)}, u32[]{:S(2)}, u32[]{:S(2)}) collective-permute-start(f32[3,4,16,128]{3,2,1,0:T(8,128)S(1)} %bitcast.38), channel_id=1, source_target_pairs={{0,90},{6,0},{12,6},{18,12},{24,18},{30,24},{36,30},{42,36},{48,42... | collective-permute-start | bytes 294920 | tf_op jit(solution)/shard_map/ppermute | solution.py:439
  72.7 15.8 %all-to-all-start.3 = ((f32[16,9,2,128]{3,2,1,0:T(2,128)}), f32[16,9,2,128]{3,2,1,0:T(2,128)S(1)}, u32[]{:S(2)}, u32[]{:S(2)}) async-start(f32[16,9,2,128]{3,2,1,0:T(2,128)} %bitcast.10), calls=%async_computation.3 | async-start | bytes 294912 | tf_op jit(solution)/shard_map/all_to_all | solution.py:435
  78.9 9.5 %copy-start = (bf16[8,256,256]{2,1,0:T(8,128)(2,1)S(1)}, bf16[8,256,256]{2,1,0:T(8,128)(2,1)}, u32[]{:S(2)}) copy-start(bf16[8,256,256]{2,1,0:T(8,128)(2,1)} %constant.40.clone.table_ref) | copy-start | bytes 3145732
  78.9 9.5 %copy-start.4 = (f32[1,1,16,3,128]{4,2,3,1,0:T(8,128)S(1)}, f32[1,1,16,3,128]{4,2,3,1,0:T(8,128)}, u32[]{:S(2)}) copy-start(f32[1,1,16,3,128]{4,2,3,1,0:T(8,128)} %param.19) | copy-start | bytes 73732
  78.9 9.5 %copy-start.11 = (f32[1,1,16,3,128]{4,2,3,1,0:T(8,128)S(1)}, f32[1,1,16,3,128]{4,2,3,1,0:T(8,128)}, u32[]{:S(2)}) copy-start(f32[1,1,16,3,128]{4,2,3,1,0:T(8,128)} %param.21) | copy-start | bytes 73732
  79.0 9.5 %copy-start.14 = (f32[16,128]{1,0:T(8,128)S(1)}, f32[16,128]{1,0:T(8,128)}, u32[]{:S(2)}) copy-start(f32[16,128]{1,0:T(8,128)} %constant.41.clone.sine_ref) | copy-start | bytes 24580
  79.0 9.5 %copy-start.15 = (f32[16,128]{1,0:T(8,128)S(1)}, f32[16,128]{1,0:T(8,128)}, u32[]{:S(2)}) copy-start(f32[16,128]{1,0:T(8,128)} %get-tuple-element.10.live_ref) | copy-start | bytes 24580

commit v2 on v1

--- a/solution.py
+++ b/solution.py
@@ -174,8 +174,10 @@
 
 
 def table_dot(high_ref, low_ref, value):
+    lanes = value.shape[1]
     high, low = split(value)
-    return dot(high_ref[...], high) + dot(high_ref[...], low) + dot(low_ref[...], high)
+    both = dot(high_ref[...], jnp.concatenate([high, low], axis=1))
+    return both[:, :lanes] + both[:, lanes:] + dot(low_ref[...], high)
 
 
 def dot_table(value, table_ref, at):
@@ -208,6 +210,7 @@
     pos_hbm,
     mass_hbm,
     table_hbm,
+    sine_hbm,
     out_ref,
     packed_ref,
     live_ref,
@@ -225,6 +228,7 @@
                 (pos_hbm, pos_ref),
                 (mass_hbm, mass_ref),
                 (table_hbm, table_ref),
+                (sine_hbm, live_ref.at[TZ : TZ + PY]),
             )
         )
     ]
@@ -242,14 +246,14 @@
         packed_ref[3, tile : tile + 1, :] = mass
         flat_high, flat_low = split(plane_weights(pos_ref, tile) * mass)
         deep_high, deep_low = split(depth_weights(pos_ref, tile))
-        windows.append(
-            dot_t(flat_high, deep_high) + dot_t(flat_high, deep_low) + dot_t(flat_low, deep_high)
-        )
+        both = dot_t(jnp.concatenate([flat_high, flat_low], axis=0), deep_high)
+        windows.append(both[:16] + both[16:] + dot_t(flat_high, deep_low))
     even = jnp.concatenate(windows[0::2], axis=1)
     odd = jnp.concatenate(windows[1::2], axis=1)
     density = pltpu.roll(even, NZ - CELLS // 2, 1) + pltpu.roll(odd, CELLS // 2, 1)
     pairs = waves_of([density[:, 128 * a : 128 * a + 128] for a in range(8)])
-    loads[3].wait()
+    for load in loads[3:]:
+        load.wait()
     modes = [dot_table(value, table_ref, at) for at, value in enumerate(pairs)]
     first = iota((8, 128), 1) < BLOCK
     for pair in range(PY // 2):
@@ -314,7 +318,7 @@
 
 
 def kick_kernel(
-    live_ref, in_ref, pos_ref, vel_ref, short_ref, table_ref, sine_ref, out_ref
+    live_ref, in_ref, vel_ref, short_ref, deep_ref, flat_ref, table_ref, out_ref
 ):
     first = iota((24, 128), 1) < BLOCK
     cosines = (iota((8, 128), 1) & (BLOCK - 1)) < HALF
@@ -328,7 +332,7 @@
         turned = jnp.where(
             cosines, pltpu.roll(parts[2], 128 - HALF, 1), pltpu.roll(parts[2], HALF, 1)
         )
-        return jnp.concatenate(parts[:2] + [turned * sine_ref[at : at + 1, :]], axis=0)
+        return jnp.concatenate(parts[:2] + [turned * live_ref[TZ + at : TZ + at + 1, :]], axis=0)
 
     near, far = [], []
     for pair in range(PY // 2):
@@ -349,10 +353,9 @@
         start = 128 * (tile // 2)
         window = shifted[tile % 2][:, start : start + 128]
         high, low = split(window)
-        deep_high, deep_low = split(depth_weights(pos_ref, tile))
-        both = dot(jnp.concatenate([high, low], axis=0), deep_high)
-        picked = both[:48] + both[48:] + dot(high, deep_low)
-        flat = plane_weights(pos_ref, tile)
+        both = dot(jnp.concatenate([high, low], axis=0), deep_ref[0, tile])
+        picked = both[:48] + both[48:] + dot(high, deep_ref[1, tile])
+        flat = flat_ref[tile]
         live = live_ref[tile : tile + 1, :]
         for comp in range(3):
             at = 8 * comp
@@ -362,7 +365,13 @@
             out_ref[comp, tile : tile + 1, :] = vel_ref[comp, tile : tile + 1, :] + live * kick
 
 
-def short_kernel(listed, left_ref, mid_ref, right_ref, out_ref, shell, sums_even, sums_odd):
+def short_kernel(
+    listed, left_ref, mid_ref, right_ref, out_ref, deep_ref, flat_ref, shell, sums_even, sums_odd
+):
+    pos_ref = mid_ref.at[1]
+    for tile in range(TZ):
+        flat_ref[tile] = plane_weights(pos_ref, tile)
+        deep_ref[0, tile], deep_ref[1, tile] = split(depth_weights(pos_ref, tile))
     for at, ref in enumerate((left_ref, mid_ref, right_ref)):
         for dx in range(3):
             shell[3 * dx + at] = ref[dx]
@@ -420,9 +429,10 @@
 def call(kernel, shapes, operands, spaces="", scratch=(), cost=None, room=24 << 20):
     space_of = {"s": pltpu.SMEM, "h": pltpu.HBM, "a": pl.ANY, "v": pltpu.VMEM}
     spaces = spaces.ljust(len(operands), "v")
+    shapes = [shape if isinstance(shape[0], tuple) else (shape, f32) for shape in shapes]
     return pl.pallas_call(
         kernel,
-        out_shape=[jax.ShapeDtypeStruct(shape, f32) for shape in shapes],
+        out_shape=[jax.ShapeDtypeStruct(*shape) for shape in shapes],
         in_specs=[pl.BlockSpec(memory_space=space_of[space]) for space in spaces],
         out_specs=[pl.BlockSpec(memory_space=pltpu.VMEM)] * len(shapes),
         scratch_shapes=scratch,
@@ -441,15 +451,14 @@
 
 def short_range(*operands):
     pairs = TZ * NB * 128 * 128
-    (short,) = call(
+    return call(
         short_kernel,
-        [(3, TZ, 128)],
+        [(3, TZ, 128), ((2, TZ, 128, 128), bf16), (TZ, 16, 128)],
         operands,
         spaces="s",
         scratch=[pltpu.VMEM((9, 4, TZ, 128), f32)] + [pltpu.VMEM((3 * 128, 128), f32)] * 2,
         cost=pl.CostEstimate(flops=40_000 * pairs, bytes_accessed=400_000, transcendentals=2 * pairs),
     )
-    return short
 
 
 def shards(positions, masses, velocities, tile_counts, neighbour_list):
@@ -464,15 +473,15 @@
     tile_shape = (4, TZ, 128)
     modes, packed, live = call(
         deposit_kernel,
-        [(PY, 8, 128), tile_shape, (TZ, 128)],
-        (counts, position, mass, t["fwd_z"]),
-        spaces="hhhh",
+        [(PY, 8, 128), tile_shape, (TZ + PY, 128)],
+        (counts, position, mass, t["fwd_z"], t["sine_z"]),
+        spaces="hhhhh",
         scratch=[
             pltpu.SMEM((1, TZ), jnp.int32),
             pltpu.VMEM((3, TZ, 128), f32),
             pltpu.VMEM((TZ, 128), f32),
             pltpu.VMEM((8, 256, 256), bf16),
-            pltpu.SemaphoreType.DMA((4,)),
+            pltpu.SemaphoreType.DMA((5,)),
         ],
         room=63_400_000,
     )
@@ -494,11 +503,11 @@
     left = shift(row, "gy", PY, 1)
     right = shift(row, "gy", PY, -1)
     fields = exchange(fields.reshape(PY, 3 * CY // 2, 2, 128), "gy").reshape(PY * 3 * CY, 128)
-    short = short_range(listed, left, row, right)
+    short, deep, flat = short_range(listed, left, row, right)
     (kicked,) = call(
         kick_kernel,
         [(3, TZ, 128)],
-        (live, fields, position, velocity, short, t["inv_z"], t["sine_z"]),
+        (live, fields, velocity, short, deep, flat, t["inv_z"]),
     )
     return jnp.transpose(kicked, (1, 0, 2))[None, None]
 

time: 90.5 us -> 87.9 us (0.971)
  starting transfers between devices: 9.89 us -> 7.91 us
    all_to_all x1, starting transfers between devices: 6.21 us -> 4.18 us  [exchange(): return lax.all_to_all(value, axis, split_axis=0, concat_axis=0, tiled=True)]
  transfers between devices with their start and end apart: 3 -> 3, of which waited for: 1 -> 1; matrix products, arithmetic and copies ran while one was open for 0% -> 0% of each run, Pallas kernels for 8% -> 9%
where the time goes in v2:
time: 87.9 us; the launch traced here: 87.4 us
  blocking collectives  64.3 us (73%)
  Pallas kernels  13.5 us (15%)
  starting transfers between devices  7.91 us (9%)
  waiting for transfers between devices  1.48 us (2%)
    all_to_all x3, blocking collectives, exchange(): return lax.all_to_all(value, axis, split_axis=0, concat_axis=0, tiled=True)  64.3 us
    pallas_call x6, Pallas kernels, call(): pl.pallas_call(kernel, out_shape=[jax.ShapeDtypeStruct(*shape) for shape...  13.5 us
    all_to_all x1, starting transfers between devices, exchange(): return lax.all_to_all(value, axis, split_axis=0, concat_axis=0, tiled=True)  4.18 us
    ppermute x2, starting transfers between devices, shift(): lax.ppermute(value, axis, [(i, (i + step) % count) for i in range(count)])  3.73 us
  transfers between devices with their start and end apart: 3, of which 1 were waited for; matrix products, arithmetic and copies ran while one was open for 0% of the time, Pallas kernels for 9%

profile of v2, /device:TPU:1, one launch (start us, length us, event | category | flops | bytes accessed | tf_op | source)
XLA Modules:
  0.0 87.4 jit_solution(8802397545256535782)
XLA Ops:
  0.0 2.5 %shard_map.181 = (f32[16,8,128]{2,1,0:T(8,128)}, f32[4,16,128]{2,1,0:T(8,128)}, f32[32,128]{1,0:T(8,128)}) custom-call(s32[1,16]{1,0:T(1,128)} %bitcast.40, f32[3,16,128]{2,1,0:T(8,128)} %bitcast.38, f32[16,128]{1,0:T(8,128)} %bitcast.39, bf16[8,256,256]{2,1,0:T(8,128)(2,1)} %constant.28.clone.table_hbm, f32[16,128]{1,0:T(8,128)} %constant.29.clone.sine_hbm), custom_call_target="tpu_custom_call" | custom-call | tf_op jit(solution)/shard_map/pallas_call | solution.py:433
  2.5 0.0 copy-start.3
  2.5 0.0 copy-start.11
  2.5 0.0 copy-start.12
  2.5 21.8 %all_to_all.20 = f32[16,8,128]{2,1,0:T(8,128)S(1)} all-to-all(f32[16,8,128]{2,1,0:T(8,128)} %get-tuple-element.14), channel_id=1, replica_groups=mesh['gx'=8,'gy'=16,'gz'=6] {'gy'}, dimensions={0} | all-to-all | bytes 131072 | tf_op jit(solution)/shard_map/all_to_all | solution.py:445
  24.3 0.0 copy-done.3
  24.3 0.0 copy-done.11
  24.3 0.0 copy-done.12
  24.3 0.0 copy-start.10
  24.3 0.0 copy-start.14
  24.3 0.2 shard_map.182
  24.5 0.0 copy-start.4
  24.5 0.0 copy-start.5
  24.5 0.0 copy-start.6
  24.5 0.0 copy-start.8
  24.6 0.0 copy-start.9
  24.6 24.8 %all_to_all.21 = f32[48,4,128]{2,1,0:T(4,128)S(1)} all-to-all(f32[48,4,128]{2,1,0:T(4,128)S(1)} %bitcast.29), channel_id=1, replica_groups=mesh['gx'=8,'gy'=16,'gz'=6] {'gx','gz'}, dimensions={0} | all-to-all | bytes 196608 | tf_op jit(solution)/shard_map/all_to_all | solution.py:445
  49.4 0.0 copy-done.10
  49.4 0.0 copy-done.14
  49.4 0.0 copy-done.4
  49.4 0.0 copy-done.5
  49.4 0.0 copy-done.6
  49.5 0.0 copy-done.8
  49.5 0.0 copy-done.9
  49.5 0.4 shard_map.183
  49.9 0.0 copy-start.1
  49.9 0.0 copy-start.2
  49.9 17.6 %all_to_all.22 = f32[48,8,128]{2,1,0:T(8,128)S(1)} all-to-all(f32[48,8,128]{2,1,0:T(8,128)S(1)} %bitcast.25), channel_id=1, replica_groups=mesh['gx'=8,'gy'=16,'gz'=6] {'gx','gz'}, dimensions={0} | all-to-all | bytes 393216 | tf_op jit(solution)/shard_map/all_to_all | solution.py:445
  67.6 0.0 copy-done.1
  67.6 0.0 copy-done.2
  67.6 1.1 %shard_map.184 = (f32[288,128]{1,0:T(8,128)}, f32[3,64,128]{2,1,0:T(8,128)S(1)}) custom-call(f32[384,128]{1,0:T(8,128)S(1)} %bitcast.26, bf16[576,96]{1,0:T(8,128)(2,1)S(1)} %copy-done.2, bf16[576,96]{1,0:T(8,128)(2,1)S(1)} %copy-done.1, f32[64,128]{1,0:T(8,128)S(1)} %bitcast.32), custom_call_target="tpu_custom_call" | custom-call | tf_op jit(solution)/shard_map/pallas_call | solution.py:433
  68.7 0.0 copy-start.15
  68.7 3.7 %collective-permute-start.1 = (f32[3,4,16,128]{3,2,1,0:T(8,128)S(1)}, f32[3,4,16,128]{3,2,1,0:T(8,128)S(1)}, u32[]{:S(2)}, u32[]{:S(2)}) collective-permute-start(f32[3,4,16,128]{3,2,1,0:T(8,128)S(1)} %bitcast.35), channel_id=1, source_target_pairs={{0,90},{6,0},{12,6},{18,12},{24,18},{30,24},{36,30},{42,36},{48,42... | collective-permute-start | bytes 294920 | tf_op jit(solution)/shard_map/ppermute | solution.py:449
  72.4 0.1 collective-permute-start
  72.4 0.0 copy-done.15
  72.4 4.2 %all-to-all-start.3 = ((f32[16,9,2,128]{3,2,1,0:T(2,128)}), f32[16,9,2,128]{3,2,1,0:T(2,128)S(1)}, u32[]{:S(2)}, u32[]{:S(2)}) async-start(f32[16,9,2,128]{3,2,1,0:T(2,128)} %bitcast.10), calls=%async_computation.3 | async-start | bytes 294912 | tf_op jit(solution)/shard_map/all_to_all | solution.py:445
  76.6 0.0 collective-permute-done.1.right_ref
  76.6 0.0 collective-permute-done.left_ref
  76.6 0.0 copy-start
  76.6 0.0 copy-start.7
  76.7 0.0 copy-start.13
  76.7 7.8 %shard_map.185 = (f32[3,16,128]{2,1,0:T(8,128)S(1)}, bf16[2,16,128,128]{3,2,1,0:T(8,128)(2,1)S(1)}, f32[16,16,128]{2,1,0:T(8,128)S(1)}) custom-call(s32[6,16]{1,0:T(8,128)S(1)} %bitcast.34, f32[3,4,16,128]{3,2,1,0:T(8,128)S(1)} %collective-permute-done.left_ref, f32[3,4,16,128]{3,2,1,0:T(8,128)S(1)} %bitcast.37, ...), custom_call_target="tpu_custom_call" | custom-call | flops 62914560000 | bytes 400000 | tf_op jit(solution)/shard_map/pallas_call | solution.py:433
  84.5 1.5 %all-to-all-done.3 = f32[16,9,2,128]{3,2,1,0:T(2,128)S(1)} async-done(((f32[16,9,2,128]{3,2,1,0:T(2,128)}), f32[16,9,2,128]{3,2,1,0:T(2,128)S(1)}, u32[]{:S(2)}, u32[]{:S(2)}) %all-to-all-start.3) | async-done | bytes 147488 | tf_op jit(solution)/shard_map/all_to_all | solution.py:445
  85.9 0.0 copy-done
  85.9 0.0 copy-done.7
  85.9 0.0 copy-done.13
  85.9 1.5 %shard_map.186 = f32[3,16,128]{2,1,0:T(8,128)} custom-call(f32[32,128]{1,0:T(8,128)S(1)} %copy-done.13, f32[288,128]{1,0:T(8,128)S(1)} %bitcast.27, f32[3,16,128]{2,1,0:T(8,128)S(1)} %bitcast.33, f32[3,16,128]{2,1,0:T(8,128)S(1)} %get-tuple-element.18.short_ref, bf16[2,16,128,128]{3,2,1,0:T(8,128)(2,1)S(1)} %get-tuple-element.19.deep_ref, ...), custom_call_target="tpu_custom_call" | custom-call | tf_op jit(solution)/shard_map/pallas_call | solution.py:433
  (1 shorter events, 0.0 us)
Async XLA Ops:
  2.5 21.8 %copy-start.3 = (f32[4,16,128]{2,1,0:T(8,128)S(1)}, f32[4,16,128]{2,1,0:T(8,128)}, u32[]{:S(2)}) copy-start(f32[4,16,128]{2,1,0:T(8,128)} %get-tuple-element.15) | copy-start | bytes 98308
  2.5 21.8 %copy-start.11 = (bf16[96,128]{1,0:T(8,128)(2,1)S(1)}, bf16[96,128]{1,0:T(8,128)(2,1)}, u32[]{:S(2)}) copy-start(bf16[96,128]{1,0:T(8,128)(2,1)} %constant.31.clone.low_ref) | copy-start | bytes 73732
  2.5 21.8 %copy-start.12 = (bf16[96,128]{1,0:T(8,128)(2,1)S(1)}, bf16[96,128]{1,0:T(8,128)(2,1)}, u32[]{:S(2)}) copy-start(bf16[96,128]{1,0:T(8,128)(2,1)} %constant.30.clone.high_ref) | copy-start | bytes 73732
  24.3 25.1 %copy-start.10 = (bf16[96,96]{1,0:T(8,128)(2,1)S(1)}, bf16[96,96]{1,0:T(8,128)(2,1)}, u32[]{:S(2)}) copy-start(bf16[96,96]{1,0:T(8,128)(2,1)} %constant.32.clone.fwd_high) | copy-start | bytes 55300
  24.3 25.1 %copy-start.14 = (f32[16,128]{1,0:T(8,128)S(1)}, f32[16,128]{1,0:T(8,128)}, u32[]{:S(2)}) copy-start(f32[16,128]{1,0:T(8,128)} %constant.38.clone.kappa_z) | copy-start | bytes 24580
  24.5 24.9 %copy-start.4 = (f32[96,1]{1,0:T(8,128)S(1)}, f32[96,1]{1,0:T(8,128)}, u32[]{:S(2)}) copy-start(f32[96,1]{1,0:T(8,128)} %constant.36.clone.kappa_x) | copy-start | bytes 1156
  24.5 24.9 %copy-start.5 = (bf16[192,96]{1,0:T(8,128)(2,1)S(1)}, bf16[192,96]{1,0:T(8,128)(2,1)}, u32[]{:S(2)}) copy-start(bf16[192,96]{1,0:T(8,128)(2,1)} %constant.35.clone.inv_low) | copy-start | bytes 110596
  24.5 24.9 %copy-start.6 = (bf16[192,96]{1,0:T(8,128)(2,1)S(1)}, bf16[192,96]{1,0:T(8,128)(2,1)}, u32[]{:S(2)}) copy-start(bf16[192,96]{1,0:T(8,128)(2,1)} %constant.34.clone.inv_high) | copy-start | bytes 110596
  24.5 24.9 %copy-start.8 = (f32[48,128]{1,0:T(8,128)S(1)}, f32[48,128]{1,0:T(8,128)}, u32[]{:S(2)}) copy-start(f32[48,128]{1,0:T(8,128)} %constant.37.clone.kappa_y) | copy-start | bytes 73732
  24.6 24.9 %copy-start.9 = (bf16[96,96]{1,0:T(8,128)(2,1)S(1)}, bf16[96,96]{1,0:T(8,128)(2,1)}, u32[]{:S(2)}) copy-start(bf16[96,96]{1,0:T(8,128)(2,1)} %constant.33.clone.fwd_low) | copy-start | bytes 55300
  49.9 17.7 %copy-start.1 = (bf16[576,96]{1,0:T(8,128)(2,1)S(1)}, bf16[576,96]{1,0:T(8,128)(2,1)}, u32[]{:S(2)}) copy-start(bf16[576,96]{1,0:T(8,128)(2,1)} %constant.40.clone.low_ref) | copy-start | bytes 331780
  49.9 17.7 %copy-start.2 = (bf16[576,96]{1,0:T(8,128)(2,1)S(1)}, bf16[576,96]{1,0:T(8,128)(2,1)}, u32[]{:S(2)}) copy-start(bf16[576,96]{1,0:T(8,128)(2,1)} %constant.39.clone.high_ref) | copy-start | bytes 331780
  68.7 3.7 %copy-start.15 = (s32[1,1,16,6]{2,1,3,0:T(1,128)S(1)}, s32[1,1,16,6]{2,1,3,0:T(1,128)}, u32[]{:S(2)}) copy-start(s32[1,1,16,6]{2,1,3,0:T(1,128)} %param.23) | copy-start | bytes 1156
  68.7 7.9 %collective-permute-start.1 = (f32[3,4,16,128]{3,2,1,0:T(8,128)S(1)}, f32[3,4,16,128]{3,2,1,0:T(8,128)S(1)}, u32[]{:S(2)}, u32[]{:S(2)}) collective-permute-start(f32[3,4,16,128]{3,2,1,0:T(8,128)S(1)} %bitcast.35), channel_id=1, source_target_pairs={{0,90},{6,0},{12,6},{18,12},{24,18},{30,24},{36,30},{42,36},{48,42... | collective-permute-start | bytes 294920 | tf_op jit(solution)/shard_map/ppermute | solution.py:449
  72.4 4.3 %collective-permute-start = (f32[3,4,16,128]{3,2,1,0:T(8,128)S(1)}, f32[3,4,16,128]{3,2,1,0:T(8,128)S(1)}, u32[]{:S(2)}, u32[]{:S(2)}) collective-permute-start(f32[3,4,16,128]{3,2,1,0:T(8,128)S(1)} %bitcast.36), channel_id=1, source_target_pairs={{0,6},{6,12},{12,18},{18,24},{24,30},{30,36},{36,42},{42,48},{48,5... | collective-permute-start | bytes 294920 | tf_op jit(solution)/shard_map/ppermute | solution.py:449
  72.4 13.5 %all-to-all-start.3 = ((f32[16,9,2,128]{3,2,1,0:T(2,128)}), f32[16,9,2,128]{3,2,1,0:T(2,128)S(1)}, u32[]{:S(2)}, u32[]{:S(2)}) async-start(f32[16,9,2,128]{3,2,1,0:T(2,128)} %bitcast.10), calls=%async_computation.3 | async-start | bytes 294912 | tf_op jit(solution)/shard_map/all_to_all | solution.py:445
  76.6 9.3 %copy-start = (bf16[8,256,256]{2,1,0:T(8,128)(2,1)S(1)}, bf16[8,256,256]{2,1,0:T(8,128)(2,1)}, u32[]{:S(2)}) copy-start(bf16[8,256,256]{2,1,0:T(8,128)(2,1)} %constant.41.clone.table_ref) | copy-start | bytes 3145732
  76.6 9.3 %copy-start.7 = (f32[1,1,16,3,128]{4,2,3,1,0:T(8,128)S(1)}, f32[1,1,16,3,128]{4,2,3,1,0:T(8,128)}, u32[]{:S(2)}) copy-start(f32[1,1,16,3,128]{4,2,3,1,0:T(8,128)} %param.21) | copy-start | bytes 73732
  76.7 9.3 %copy-start.13 = (f32[32,128]{1,0:T(8,128)S(1)}, f32[32,128]{1,0:T(8,128)}, u32[]{:S(2)}) copy-start(f32[32,128]{1,0:T(8,128)} %get-tuple-element.13.live_ref) | copy-start | bytes 49156

commit v3 on v2

--- a/solution.py
+++ b/solution.py
@@ -21,7 +21,7 @@
 CELLS = NZ // TZ
 BLOCK = NZ // PY
 HALF = BLOCK // 2
-PIECES = 4 * TZ // 2
+REST = 4 * TZ - PX
 
 smoothing = 0.1
 screening = 0.01
@@ -140,9 +140,7 @@
     out = {}
     out["fwd_z"] = np.concatenate(halves(table_z), axis=0)
     out["inv_z"] = np.concatenate(halves(table_z.transpose(0, 2, 1)), axis=0)
-    pad_y = np.zeros((2, PX, PY, 8))
-    pad_y[..., :CY] = basis_y.T.reshape(PX, 2, PY, CY).transpose(1, 0, 2, 3)
-    out["fwd_y"] = halves(pad_y.reshape(NY, PY * 8))
+    out["fwd_y"] = halves(basis_y.T.reshape(PX, 2, NY).transpose(1, 0, 2).reshape(NY, NY))
     out["fwd_x"] = halves(basis_x.reshape(PX, CX, NX).transpose(2, 1, 0).reshape(NX, CX * PX))
     both = np.stack([slope_x.reshape(PX, CX, NX), basis_x.reshape(PX, CX, NX)])
     out["inv_x"] = halves(both.transpose(0, 2, 1, 3).reshape(2 * CX * PX, NX))
@@ -260,18 +258,22 @@
         part = modes[pair // 2][:, 128 * (pair % 2) : 128 * (pair % 2) + 128]
         near = part[:8]
         far = part[8:]
-        out_ref[2 * pair] = jnp.where(first, near, pltpu.roll(far, BLOCK, 1))
-        out_ref[2 * pair + 1] = jnp.where(first, pltpu.roll(near, BLOCK, 1), far)
+        blocks = (
+            jnp.where(first, near, pltpu.roll(far, BLOCK, 1)),
+            jnp.where(first, pltpu.roll(near, BLOCK, 1), far),
+        )
+        for at, block in enumerate(blocks):
+            start = CY * (2 * pair + at)
+            out_ref[start : start + CY, :] = block[:CY]
 
 
 def forward_y_kernel(in_ref, high_ref, low_ref, packed_ref, out_ref):
     value = table_dot(high_ref, low_ref, in_ref[...])
     for at in range(2):
         out_ref[pl.ds(at, PX, stride=4), :] = value[PX * at : PX * (at + 1)]
-        out_ref[pl.ds(2 + at, PIECES, stride=4), :] = packed_ref[pl.ds(at, PIECES, stride=2), :]
-        out_ref[pl.ds(4 * PIECES + 2 + at, PX - PIECES, stride=4), :] = jnp.zeros(
-            (PX - PIECES, 128), f32
-        )
+        out_ref[pl.ds(3 + 4 * at, REST, stride=8), :] = packed_ref[PX:, :]
+    out_ref[pl.ds(2, PX, stride=4), :] = packed_ref[:PX, :]
+    out_ref[pl.ds(8 * REST + 3, PX - 2 * REST, stride=4), :] = jnp.zeros((PX - 2 * REST, 128), f32)
 
 
 def solve_x_kernel(
@@ -289,18 +291,25 @@
     potential = spectrum * (-jnp.exp(-smoothing * kappa_sum) / (kappa_sum + screening))
     fields = table_dot(inv_high, inv_low, potential)
     for at in range(4):
-        out_ref[pl.ds(at, PX, stride=8), :] = fields[PX * at : PX * (at + 1)]
-    for at in range(2):
-        piece = in_ref[pl.ds(2 + at, PX, stride=4), :]
-        out_ref[pl.ds(4 + at, PX, stride=8), :] = pltpu.roll(piece, 1, 0)
-        out_ref[pl.ds(6 + at, PX, stride=8), :] = pltpu.roll(piece, PX - 1, 0)
+        out_ref[pl.ds(at, PX, stride=7), :] = fields[PX * at : PX * (at + 1)]
+    piece = in_ref[pl.ds(2, PX, stride=4), :]
+    out_ref[pl.ds(4, PX, stride=7), :] = pltpu.roll(piece, 1, 0)
+    out_ref[pl.ds(5, PX, stride=7), :] = pltpu.roll(piece, PX - 1, 0)
+    near = in_ref[pl.ds(3, PX, stride=4), :]
+    far = pltpu.roll(near, BLOCK, 1)
+    even = at_x % 2 == 0
+    out_ref[pl.ds(6, PX, stride=7), :] = jnp.where(
+        first,
+        pltpu.roll(jnp.where(even, near, far), 1, 0),
+        pltpu.roll(jnp.where(even, far, near), PX - 1, 0),
+    )
 
 
 def inverse_y_kernel(in_ref, high_ref, low_ref, packed_ref, out_ref, row_ref):
     rows = PY * 3 * CY
     first = iota((rows, 128), 1) < BLOCK
     cells = [
-        jnp.concatenate([in_ref[pl.ds(at, PX, stride=8), :] for at in (x, x + 2)], axis=0)
+        jnp.concatenate([in_ref[pl.ds(at, PX, stride=7), :] for at in (x, x + 2)], axis=0)
         for x in range(CX)
     ]
     value = table_dot(high_ref, low_ref, jnp.concatenate(cells, axis=1))
@@ -310,11 +319,12 @@
     cell_1 = pltpu.roll(cos_1, BLOCK, 1) + sin_1
     out_ref[...] = jnp.where(first, cell_0, cell_1)
     row_ref[1] = packed_ref[...]
-    for at in range(2):
-        for side in range(2):
-            row_ref[2 * side, pl.ds(at, PIECES, stride=2), :] = in_ref[
-                pl.ds(4 + 2 * side + at, PIECES, stride=8), :
-            ]
+    row_ref[0, :PX, :] = in_ref[pl.ds(4, PX, stride=7), :]
+    row_ref[2, :PX, :] = in_ref[pl.ds(5, PX, stride=7), :]
+    low_half = first[:REST]
+    one, two = in_ref[pl.ds(6, REST, stride=14), :], in_ref[pl.ds(13, REST, stride=14), :]
+    row_ref[0, PX:, :] = jnp.where(low_half, one, pltpu.roll(two, BLOCK, 1))
+    row_ref[2, PX:, :] = jnp.where(low_half, pltpu.roll(one, BLOCK, 1), two)
 
 
 def kick_kernel(
@@ -473,7 +483,7 @@
     tile_shape = (4, TZ, 128)
     modes, packed, live = call(
         deposit_kernel,
-        [(PY, 8, 128), tile_shape, (TZ + PY, 128)],
+        [(NY, 128), tile_shape, (TZ + PY, 128)],
         (counts, position, mass, t["fwd_z"], t["sine_z"]),
         spaces="hhhhh",
         scratch=[
@@ -485,15 +495,15 @@
         ],
         room=63_400_000,
     )
-    modes = exchange(modes, "gy").reshape(PY * 8, 128)
+    modes = exchange(modes.reshape(PY, CY // 2, 2, 128), "gy").reshape(NY, 128)
     packed = packed.reshape(4 * TZ, 128)
     (modes,) = call(forward_y_kernel, [(4 * PX, 128)], (modes, *t["fwd_y"], packed))
     modes = exchange(modes.reshape(PX, 4, 128), wide).reshape(4 * PX, 128)
     waves = (t["kappa_x"], t["kappa_y"], t["kappa_z"])
     (fields,) = call(
-        solve_x_kernel, [(8 * PX, 128)], (modes, *t["fwd_x"], *t["inv_x"], *waves)
-    )
-    fields = exchange(fields.reshape(PX, 8, 128), wide).reshape(8 * PX, 128)
+        solve_x_kernel, [(7 * PX, 128)], (modes, *t["fwd_x"], *t["inv_x"], *waves)
+    )
+    fields = exchange(fields.reshape(PX, 7, 1, 128), wide).reshape(7 * PX, 128)
     fields, row = call(
         inverse_y_kernel,
         [(PY * 3 * CY, 128), (3, 4 * TZ, 128)],

time: 87.9 us -> 86.8 us (0.987)
  blocking collectives: 64.3 us -> 63.4 us
    all_to_all x3, blocking collectives: 64.3 us -> 63.4 us  [exchange(): return lax.all_to_all(value, axis, split_axis=0, concat_axis=0, tiled=True)]
where the time goes in v3:
time: 86.8 us; the launch traced here: 86.3 us
  blocking collectives  63.4 us (73%)
  Pallas kernels  13.5 us (16%)
  starting transfers between devices  7.7 us (9%)
  waiting for transfers between devices  1.48 us (2%)
    all_to_all x3, blocking collectives, exchange(): return lax.all_to_all(value, axis, split_axis=0, concat_axis=0, tiled=True)  63.4 us
    pallas_call x6, Pallas kernels, call(): pl.pallas_call(kernel, out_shape=[jax.ShapeDtypeStruct(*shape) for shape...  13.5 us
    all_to_all x1, starting transfers between devices, exchange(): return lax.all_to_all(value, axis, split_axis=0, concat_axis=0, tiled=True)  4.13 us
    ppermute x2, starting transfers between devices, shift(): lax.ppermute(value, axis, [(i, (i + step) % count) for i in range(count)])  3.57 us
  transfers between devices with their start and end apart: 3, of which 1 were waited for; matrix products, arithmetic and copies ran while one was open for 0% of the time, Pallas kernels for 9%

profile of v3, /device:TPU:1, one launch (start us, length us, event | category | flops | bytes accessed | tf_op | source)
XLA Modules:
  0.0 86.3 jit_solution(3937520834887903193)
XLA Ops:
  0.0 2.5 %shard_map.181 = (f32[96,128]{1,0:T(8,128)}, f32[4,16,128]{2,1,0:T(8,128)}, f32[32,128]{1,0:T(8,128)}) custom-call(s32[1,16]{1,0:T(1,128)} %bitcast.42, f32[3,16,128]{2,1,0:T(8,128)} %bitcast.40, f32[16,128]{1,0:T(8,128)} %bitcast.41, bf16[8,256,256]{2,1,0:T(8,128)(2,1)} %constant.28.clone.table_hbm, f32[16,128]{1,0:T(8,128)} %constant.29.clone.sine_hbm), custom_call_target="tpu_custom_call" | custom-call | tf_op jit(solution)/shard_map/pallas_call | solution.py:443
  2.5 0.0 copy-start.3
  2.5 0.0 copy-start.11
  2.5 0.0 copy-start.12
  2.5 21.4 %all_to_all.20 = f32[16,3,2,128]{3,2,1,0:T(2,128)S(1)} all-to-all(f32[16,3,2,128]{3,2,1,0:T(2,128)} %bitcast.39), channel_id=1, replica_groups=mesh['gx'=8,'gy'=16,'gz'=6] {'gy'}, dimensions={0} | all-to-all | bytes 98304 | tf_op jit(solution)/shard_map/all_to_all | solution.py:455
  24.0 0.0 copy-done.3
  24.0 0.0 copy-done.11
  24.0 0.0 copy-done.12
  24.0 0.0 copy-start.10
  24.0 0.0 copy-start.14
  24.0 0.2 shard_map.182
  24.2 0.0 copy-start.4
  24.2 0.0 copy-start.5
  24.2 0.0 copy-start.6
  24.2 0.0 copy-start.8
  24.2 0.0 copy-start.9
  24.2 24.6 %all_to_all.21 = f32[48,4,128]{2,1,0:T(4,128)S(1)} all-to-all(f32[48,4,128]{2,1,0:T(4,128)S(1)} %bitcast.29), channel_id=1, replica_groups=mesh['gx'=8,'gy'=16,'gz'=6] {'gx','gz'}, dimensions={0} | all-to-all | bytes 196608 | tf_op jit(solution)/shard_map/all_to_all | solution.py:455
  48.9 0.0 copy-done.10
  48.9 0.0 copy-done.14
  48.9 0.0 copy-done.4
  48.9 0.0 copy-done.5
  48.9 0.0 copy-done.6
  48.9 0.0 copy-done.8
  48.9 0.0 copy-done.9
  48.9 0.4 shard_map.183
  49.3 0.0 copy-start.1
  49.4 0.0 copy-start.2
  49.4 17.3 %all_to_all.22 = f32[48,7,1,128]{3,2,1,0:T(1,128)S(1)} all-to-all(f32[48,7,1,128]{3,2,1,0:T(1,128)S(1)} %bitcast.26), channel_id=1, replica_groups=mesh['gx'=8,'gy'=16,'gz'=6] {'gx','gz'}, dimensions={0} | all-to-all | bytes 344064 | tf_op jit(solution)/shard_map/all_to_all | solution.py:455
  66.6 0.0 copy-done.1
  66.6 0.0 copy-done.2
  66.7 1.1 %shard_map.184 = (f32[288,128]{1,0:T(8,128)}, f32[3,64,128]{2,1,0:T(8,128)S(1)}) custom-call(f32[336,128]{1,0:T(8,128)S(1)} %bitcast.27, bf16[576,96]{1,0:T(8,128)(2,1)S(1)} %copy-done.2, bf16[576,96]{1,0:T(8,128)(2,1)S(1)} %copy-done.1, f32[64,128]{1,0:T(8,128)S(1)} %bitcast.33), custom_call_target="tpu_custom_call" | custom-call | tf_op jit(solution)/shard_map/pallas_call | solution.py:443
  67.8 0.0 copy-start.15
  67.8 3.5 %collective-permute-start.1 = (f32[3,4,16,128]{3,2,1,0:T(8,128)S(1)}, f32[3,4,16,128]{3,2,1,0:T(8,128)S(1)}, u32[]{:S(2)}, u32[]{:S(2)}) collective-permute-start(f32[3,4,16,128]{3,2,1,0:T(8,128)S(1)} %bitcast.36), channel_id=1, source_target_pairs={{0,90},{6,0},{12,6},{18,12},{24,18},{30,24},{36,30},{42,36},{48,42... | collective-permute-start | bytes 294920 | tf_op jit(solution)/shard_map/ppermute | solution.py:459
  71.2 0.1 collective-permute-start
  71.3 0.0 copy-done.15
  71.3 4.1 %all-to-all-start.3 = ((f32[16,9,2,128]{3,2,1,0:T(2,128)}), f32[16,9,2,128]{3,2,1,0:T(2,128)S(1)}, u32[]{:S(2)}, u32[]{:S(2)}) async-start(f32[16,9,2,128]{3,2,1,0:T(2,128)} %bitcast.11), calls=%async_computation.3 | async-start | bytes 294912 | tf_op jit(solution)/shard_map/all_to_all | solution.py:455
  75.5 0.0 collective-permute-done.1.right_ref
  75.5 0.0 collective-permute-done.left_ref
  75.5 0.0 copy-start
  75.5 0.0 copy-start.7
  75.5 0.0 copy-start.13
  75.5 7.8 %shard_map.185 = (f32[3,16,128]{2,1,0:T(8,128)S(1)}, bf16[2,16,128,128]{3,2,1,0:T(8,128)(2,1)S(1)}, f32[16,16,128]{2,1,0:T(8,128)S(1)}) custom-call(s32[6,16]{1,0:T(8,128)S(1)} %bitcast.35, f32[3,4,16,128]{3,2,1,0:T(8,128)S(1)} %collective-permute-done.left_ref, f32[3,4,16,128]{3,2,1,0:T(8,128)S(1)} %bitcast.38, ...), custom_call_target="tpu_custom_call" | custom-call | flops 62914560000 | bytes 400000 | tf_op jit(solution)/shard_map/pallas_call | solution.py:443
  83.3 1.5 %all-to-all-done.3 = f32[16,9,2,128]{3,2,1,0:T(2,128)S(1)} async-done(((f32[16,9,2,128]{3,2,1,0:T(2,128)}), f32[16,9,2,128]{3,2,1,0:T(2,128)S(1)}, u32[]{:S(2)}, u32[]{:S(2)}) %all-to-all-start.3) | async-done | bytes 147488 | tf_op jit(solution)/shard_map/all_to_all | solution.py:455
  84.8 0.0 copy-done
  84.8 0.0 copy-done.7
  84.8 0.0 copy-done.13
  84.8 1.5 %shard_map.186 = f32[3,16,128]{2,1,0:T(8,128)} custom-call(f32[32,128]{1,0:T(8,128)S(1)} %copy-done.13, f32[288,128]{1,0:T(8,128)S(1)} %bitcast.28, f32[3,16,128]{2,1,0:T(8,128)S(1)} %bitcast.34, f32[3,16,128]{2,1,0:T(8,128)S(1)} %get-tuple-element.18.short_ref, bf16[2,16,128,128]{3,2,1,0:T(8,128)(2,1)S(1)} %get-tuple-element.19.deep_ref, ...), custom_call_target="tpu_custom_call" | custom-call | tf_op jit(solution)/shard_map/pallas_call | solution.py:443
  (1 shorter events, 0.0 us)
Async XLA Ops:
  2.5 21.5 %copy-start.3 = (f32[4,16,128]{2,1,0:T(8,128)S(1)}, f32[4,16,128]{2,1,0:T(8,128)}, u32[]{:S(2)}) copy-start(f32[4,16,128]{2,1,0:T(8,128)} %get-tuple-element.15) | copy-start | bytes 98308
  2.5 21.5 %copy-start.11 = (bf16[96,96]{1,0:T(8,128)(2,1)S(1)}, bf16[96,96]{1,0:T(8,128)(2,1)}, u32[]{:S(2)}) copy-start(bf16[96,96]{1,0:T(8,128)(2,1)} %constant.31.clone.low_ref) | copy-start | bytes 55300
  2.5 21.5 %copy-start.12 = (bf16[96,96]{1,0:T(8,128)(2,1)S(1)}, bf16[96,96]{1,0:T(8,128)(2,1)}, u32[]{:S(2)}) copy-start(bf16[96,96]{1,0:T(8,128)(2,1)} %constant.30.clone.high_ref) | copy-start | bytes 55300
  24.0 24.9 %copy-start.10 = (bf16[96,96]{1,0:T(8,128)(2,1)S(1)}, bf16[96,96]{1,0:T(8,128)(2,1)}, u32[]{:S(2)}) copy-start(bf16[96,96]{1,0:T(8,128)(2,1)} %constant.32.clone.fwd_high) | copy-start | bytes 55300
  24.0 24.9 %copy-start.14 = (f32[16,128]{1,0:T(8,128)S(1)}, f32[16,128]{1,0:T(8,128)}, u32[]{:S(2)}) copy-start(f32[16,128]{1,0:T(8,128)} %constant.38.clone.kappa_z) | copy-start | bytes 24580
  24.2 24.7 %copy-start.4 = (f32[96,1]{1,0:T(8,128)S(1)}, f32[96,1]{1,0:T(8,128)}, u32[]{:S(2)}) copy-start(f32[96,1]{1,0:T(8,128)} %constant.36.clone.kappa_x) | copy-start | bytes 1156
  24.2 24.7 %copy-start.5 = (bf16[192,96]{1,0:T(8,128)(2,1)S(1)}, bf16[192,96]{1,0:T(8,128)(2,1)}, u32[]{:S(2)}) copy-start(bf16[192,96]{1,0:T(8,128)(2,1)} %constant.35.clone.inv_low) | copy-start | bytes 110596
  24.2 24.7 %copy-start.6 = (bf16[192,96]{1,0:T(8,128)(2,1)S(1)}, bf16[192,96]{1,0:T(8,128)(2,1)}, u32[]{:S(2)}) copy-start(bf16[192,96]{1,0:T(8,128)(2,1)} %constant.34.clone.inv_high) | copy-start | bytes 110596
  24.2 24.7 %copy-start.8 = (f32[48,128]{1,0:T(8,128)S(1)}, f32[48,128]{1,0:T(8,128)}, u32[]{:S(2)}) copy-start(f32[48,128]{1,0:T(8,128)} %constant.37.clone.kappa_y) | copy-start | bytes 73732
  24.2 24.7 %copy-start.9 = (bf16[96,96]{1,0:T(8,128)(2,1)S(1)}, bf16[96,96]{1,0:T(8,128)(2,1)}, u32[]{:S(2)}) copy-start(bf16[96,96]{1,0:T(8,128)(2,1)} %constant.33.clone.fwd_low) | copy-start | bytes 55300
  49.3 17.3 %copy-start.1 = (bf16[576,96]{1,0:T(8,128)(2,1)S(1)}, bf16[576,96]{1,0:T(8,128)(2,1)}, u32[]{:S(2)}) copy-start(bf16[576,96]{1,0:T(8,128)(2,1)} %constant.40.clone.low_ref) | copy-start | bytes 331780
  49.4 17.3 %copy-start.2 = (bf16[576,96]{1,0:T(8,128)(2,1)S(1)}, bf16[576,96]{1,0:T(8,128)(2,1)}, u32[]{:S(2)}) copy-start(bf16[576,96]{1,0:T(8,128)(2,1)} %constant.39.clone.high_ref) | copy-start | bytes 331780
  67.8 3.6 %copy-start.15 = (s32[1,1,16,6]{2,1,3,0:T(1,128)S(1)}, s32[1,1,16,6]{2,1,3,0:T(1,128)}, u32[]{:S(2)}) copy-start(s32[1,1,16,6]{2,1,3,0:T(1,128)} %param.23) | copy-start | bytes 1156
  67.8 7.7 %collective-permute-start.1 = (f32[3,4,16,128]{3,2,1,0:T(8,128)S(1)}, f32[3,4,16,128]{3,2,1,0:T(8,128)S(1)}, u32[]{:S(2)}, u32[]{:S(2)}) collective-permute-start(f32[3,4,16,128]{3,2,1,0:T(8,128)S(1)} %bitcast.36), channel_id=1, source_target_pairs={{0,90},{6,0},{12,6},{18,12},{24,18},{30,24},{36,30},{42,36},{48,42... | collective-permute-start | bytes 294920 | tf_op jit(solution)/shard_map/ppermute | solution.py:459
  71.2 4.3 %collective-permute-start = (f32[3,4,16,128]{3,2,1,0:T(8,128)S(1)}, f32[3,4,16,128]{3,2,1,0:T(8,128)S(1)}, u32[]{:S(2)}, u32[]{:S(2)}) collective-permute-start(f32[3,4,16,128]{3,2,1,0:T(8,128)S(1)} %bitcast.37), channel_id=1, source_target_pairs={{0,6},{6,12},{12,18},{18,24},{24,30},{30,36},{36,42},{42,48},{48,5... | collective-permute-start | bytes 294920 | tf_op jit(solution)/shard_map/ppermute | solution.py:459
  71.3 13.5 %all-to-all-start.3 = ((f32[16,9,2,128]{3,2,1,0:T(2,128)}), f32[16,9,2,128]{3,2,1,0:T(2,128)S(1)}, u32[]{:S(2)}, u32[]{:S(2)}) async-start(f32[16,9,2,128]{3,2,1,0:T(2,128)} %bitcast.11), calls=%async_computation.3 | async-start | bytes 294912 | tf_op jit(solution)/shard_map/all_to_all | solution.py:455
  75.5 9.3 %copy-start = (bf16[8,256,256]{2,1,0:T(8,128)(2,1)S(1)}, bf16[8,256,256]{2,1,0:T(8,128)(2,1)}, u32[]{:S(2)}) copy-start(bf16[8,256,256]{2,1,0:T(8,128)(2,1)} %constant.41.clone.table_ref) | copy-start | bytes 3145732
  75.5 9.3 %copy-start.7 = (f32[1,1,16,3,128]{4,2,3,1,0:T(8,128)S(1)}, f32[1,1,16,3,128]{4,2,3,1,0:T(8,128)}, u32[]{:S(2)}) copy-start(f32[1,1,16,3,128]{4,2,3,1,0:T(8,128)} %param.21) | copy-start | bytes 73732
  75.5 9.3 %copy-start.13 = (f32[32,128]{1,0:T(8,128)S(1)}, f32[32,128]{1,0:T(8,128)}, u32[]{:S(2)}) copy-start(f32[32,128]{1,0:T(8,128)} %get-tuple-element.13.live_ref) | copy-start | bytes 49156

commit v4 on v3

--- a/solution.py
+++ b/solution.py
@@ -107,6 +107,7 @@
 
 
 ROOT_HALF = float(np.sqrt(0.5))
+EXPONENT = float(-np.log2(np.e) / split_scale)
 
 
 def waves_of(cells):
@@ -408,7 +409,7 @@
                 apart = [x - own[0], y - own[1], z - own[2]]
                 square = apart[0] * apart[0] + apart[1] * apart[1] + apart[2] * apart[2]
                 root = lax.rsqrt(square + softening)
-                strength = (mass * jnp.exp(square * (-1.0 / split_scale))) * (root * root * root)
+                strength = (mass * jnp.exp2(square * EXPONENT)) * (root * root * root)
                 for comp in range(3):
                     term = strength * apart[comp]
                     totals[comp] = term if totals[comp] is None else totals[comp] + term

time: 86.8 us -> 86.8 us (level)
  no operation moved by 1% of the time
where the time goes in v4:
time: 86.8 us; the launch traced here: 86.3 us
  blocking collectives  63.4 us (73%)
  Pallas kernels  13.3 us (15%)
  starting transfers between devices  7.7 us (9%)
  waiting for transfers between devices  1.67 us (2%)
    all_to_all x3, blocking collectives, exchange(): return lax.all_to_all(value, axis, split_axis=0, concat_axis=0, tiled=True)  63.4 us
    pallas_call x6, Pallas kernels, call(): pl.pallas_call(kernel, out_shape=[jax.ShapeDtypeStruct(*shape) for shape...  13.3 us
    all_to_all x1, starting transfers between devices, exchange(): return lax.all_to_all(value, axis, split_axis=0, concat_axis=0, tiled=True)  4.13 us
    ppermute x2, starting transfers between devices, shift(): lax.ppermute(value, axis, [(i, (i + step) % count) for i in range(count)])  3.57 us
  transfers between devices with their start and end apart: 3, of which 1 were waited for; matrix products, arithmetic and copies ran while one was open for 0% of the time, Pallas kernels for 9%

profile of v4, /device:TPU:1, one launch (start us, length us, event | category | flops | bytes accessed | tf_op | source)
XLA Modules:
  0.0 86.3 jit_solution(9980638749170830666)
XLA Ops:
  0.0 2.5 %shard_map.181 = (f32[96,128]{1,0:T(8,128)}, f32[4,16,128]{2,1,0:T(8,128)}, f32[32,128]{1,0:T(8,128)}) custom-call(s32[1,16]{1,0:T(1,128)} %bitcast.42, f32[3,16,128]{2,1,0:T(8,128)} %bitcast.40, f32[16,128]{1,0:T(8,128)} %bitcast.41, bf16[8,256,256]{2,1,0:T(8,128)(2,1)} %constant.28.clone.table_hbm, f32[16,128]{1,0:T(8,128)} %constant.29.clone.sine_hbm), custom_call_target="tpu_custom_call" | custom-call | tf_op jit(solution)/shard_map/pallas_call | solution.py:444
  2.5 0.0 copy-start.3
  2.5 0.0 copy-start.11
  2.5 0.0 copy-start.12
  2.5 21.4 %all_to_all.20 = f32[16,3,2,128]{3,2,1,0:T(2,128)S(1)} all-to-all(f32[16,3,2,128]{3,2,1,0:T(2,128)} %bitcast.39), channel_id=1, replica_groups=mesh['gx'=8,'gy'=16,'gz'=6] {'gy'}, dimensions={0} | all-to-all | bytes 98304 | tf_op jit(solution)/shard_map/all_to_all | solution.py:456
  24.0 0.0 copy-done.3
  24.0 0.0 copy-done.11
  24.0 0.0 copy-done.12
  24.0 0.0 copy-start.10
  24.0 0.0 copy-start.14
  24.0 0.2 shard_map.182
  24.2 0.0 copy-start.4
  24.2 0.0 copy-start.5
  24.2 0.0 copy-start.6
  24.2 0.0 copy-start.8
  24.2 0.0 copy-start.9
  24.2 24.6 %all_to_all.21 = f32[48,4,128]{2,1,0:T(4,128)S(1)} all-to-all(f32[48,4,128]{2,1,0:T(4,128)S(1)} %bitcast.29), channel_id=1, replica_groups=mesh['gx'=8,'gy'=16,'gz'=6] {'gx','gz'}, dimensions={0} | all-to-all | bytes 196608 | tf_op jit(solution)/shard_map/all_to_all | solution.py:456
  48.9 0.0 copy-done.10
  48.9 0.0 copy-done.14
  48.9 0.0 copy-done.4
  48.9 0.0 copy-done.5
  48.9 0.0 copy-done.6
  48.9 0.0 copy-done.8
  48.9 0.0 copy-done.9
  48.9 0.4 shard_map.183
  49.3 0.0 copy-start.1
  49.4 0.0 copy-start.2
  49.4 17.3 %all_to_all.22 = f32[48,7,1,128]{3,2,1,0:T(1,128)S(1)} all-to-all(f32[48,7,1,128]{3,2,1,0:T(1,128)S(1)} %bitcast.26), channel_id=1, replica_groups=mesh['gx'=8,'gy'=16,'gz'=6] {'gx','gz'}, dimensions={0} | all-to-all | bytes 344064 | tf_op jit(solution)/shard_map/all_to_all | solution.py:456
  66.6 0.0 copy-done.1
  66.6 0.0 copy-done.2
  66.7 1.1 %shard_map.184 = (f32[288,128]{1,0:T(8,128)}, f32[3,64,128]{2,1,0:T(8,128)S(1)}) custom-call(f32[336,128]{1,0:T(8,128)S(1)} %bitcast.27, bf16[576,96]{1,0:T(8,128)(2,1)S(1)} %copy-done.2, bf16[576,96]{1,0:T(8,128)(2,1)S(1)} %copy-done.1, f32[64,128]{1,0:T(8,128)S(1)} %bitcast.33), custom_call_target="tpu_custom_call" | custom-call | tf_op jit(solution)/shard_map/pallas_call | solution.py:444
  67.8 0.0 copy-start.15
  67.8 3.5 %collective-permute-start.1 = (f32[3,4,16,128]{3,2,1,0:T(8,128)S(1)}, f32[3,4,16,128]{3,2,1,0:T(8,128)S(1)}, u32[]{:S(2)}, u32[]{:S(2)}) collective-permute-start(f32[3,4,16,128]{3,2,1,0:T(8,128)S(1)} %bitcast.36), channel_id=1, source_target_pairs={{0,90},{6,0},{12,6},{18,12},{24,18},{30,24},{36,30},{42,36},{48,42... | collective-permute-start | bytes 294920 | tf_op jit(solution)/shard_map/ppermute | solution.py:460
  71.2 0.1 collective-permute-start
  71.3 0.0 copy-done.15
  71.3 4.1 %all-to-all-start.3 = ((f32[16,9,2,128]{3,2,1,0:T(2,128)}), f32[16,9,2,128]{3,2,1,0:T(2,128)S(1)}, u32[]{:S(2)}, u32[]{:S(2)}) async-start(f32[16,9,2,128]{3,2,1,0:T(2,128)} %bitcast.11), calls=%async_computation.3 | async-start | bytes 294912 | tf_op jit(solution)/shard_map/all_to_all | solution.py:456
  75.5 0.0 collective-permute-done.1.right_ref
  75.5 0.0 collective-permute-done.left_ref
  75.5 0.0 copy-start
  75.5 0.0 copy-start.7
  75.5 0.0 copy-start.13
  75.5 7.6 %shard_map.185 = (f32[3,16,128]{2,1,0:T(8,128)S(1)}, bf16[2,16,128,128]{3,2,1,0:T(8,128)(2,1)S(1)}, f32[16,16,128]{2,1,0:T(8,128)S(1)}) custom-call(s32[6,16]{1,0:T(8,128)S(1)} %bitcast.35, f32[3,4,16,128]{3,2,1,0:T(8,128)S(1)} %collective-permute-done.left_ref, f32[3,4,16,128]{3,2,1,0:T(8,128)S(1)} %bitcast.38, ...), custom_call_target="tpu_custom_call" | custom-call | flops 62914560000 | bytes 400000 | tf_op jit(solution)/shard_map/pallas_call | solution.py:444
  83.1 1.7 %all-to-all-done.3 = f32[16,9,2,128]{3,2,1,0:T(2,128)S(1)} async-done(((f32[16,9,2,128]{3,2,1,0:T(2,128)}), f32[16,9,2,128]{3,2,1,0:T(2,128)S(1)}, u32[]{:S(2)}, u32[]{:S(2)}) %all-to-all-start.3) | async-done | bytes 147488 | tf_op jit(solution)/shard_map/all_to_all | solution.py:456
  84.8 0.0 copy-done
  84.8 0.0 copy-done.7
  84.8 0.0 copy-done.13
  84.8 1.5 %shard_map.186 = f32[3,16,128]{2,1,0:T(8,128)} custom-call(f32[32,128]{1,0:T(8,128)S(1)} %copy-done.13, f32[288,128]{1,0:T(8,128)S(1)} %bitcast.28, f32[3,16,128]{2,1,0:T(8,128)S(1)} %bitcast.34, f32[3,16,128]{2,1,0:T(8,128)S(1)} %get-tuple-element.18.short_ref, bf16[2,16,128,128]{3,2,1,0:T(8,128)(2,1)S(1)} %get-tuple-element.19.deep_ref, ...), custom_call_target="tpu_custom_call" | custom-call | tf_op jit(solution)/shard_map/pallas_call | solution.py:444
  (1 shorter events, 0.0 us)
Async XLA Ops:
  2.5 21.5 %copy-start.3 = (f32[4,16,128]{2,1,0:T(8,128)S(1)}, f32[4,16,128]{2,1,0:T(8,128)}, u32[]{:S(2)}) copy-start(f32[4,16,128]{2,1,0:T(8,128)} %get-tuple-element.15) | copy-start | bytes 98308
  2.5 21.5 %copy-start.11 = (bf16[96,96]{1,0:T(8,128)(2,1)S(1)}, bf16[96,96]{1,0:T(8,128)(2,1)}, u32[]{:S(2)}) copy-start(bf16[96,96]{1,0:T(8,128)(2,1)} %constant.31.clone.low_ref) | copy-start | bytes 55300
  2.5 21.5 %copy-start.12 = (bf16[96,96]{1,0:T(8,128)(2,1)S(1)}, bf16[96,96]{1,0:T(8,128)(2,1)}, u32[]{:S(2)}) copy-start(bf16[96,96]{1,0:T(8,128)(2,1)} %constant.30.clone.high_ref) | copy-start | bytes 55300
  24.0 24.9 %copy-start.10 = (bf16[96,96]{1,0:T(8,128)(2,1)S(1)}, bf16[96,96]{1,0:T(8,128)(2,1)}, u32[]{:S(2)}) copy-start(bf16[96,96]{1,0:T(8,128)(2,1)} %constant.32.clone.fwd_high) | copy-start | bytes 55300
  24.0 24.9 %copy-start.14 = (f32[16,128]{1,0:T(8,128)S(1)}, f32[16,128]{1,0:T(8,128)}, u32[]{:S(2)}) copy-start(f32[16,128]{1,0:T(8,128)} %constant.38.clone.kappa_z) | copy-start | bytes 24580
  24.2 24.7 %copy-start.4 = (f32[96,1]{1,0:T(8,128)S(1)}, f32[96,1]{1,0:T(8,128)}, u32[]{:S(2)}) copy-start(f32[96,1]{1,0:T(8,128)} %constant.36.clone.kappa_x) | copy-start | bytes 1156
  24.2 24.7 %copy-start.5 = (bf16[192,96]{1,0:T(8,128)(2,1)S(1)}, bf16[192,96]{1,0:T(8,128)(2,1)}, u32[]{:S(2)}) copy-start(bf16[192,96]{1,0:T(8,128)(2,1)} %constant.35.clone.inv_low) | copy-start | bytes 110596
  24.2 24.7 %copy-start.6 = (bf16[192,96]{1,0:T(8,128)(2,1)S(1)}, bf16[192,96]{1,0:T(8,128)(2,1)}, u32[]{:S(2)}) copy-start(bf16[192,96]{1,0:T(8,128)(2,1)} %constant.34.clone.inv_high) | copy-start | bytes 110596
  24.2 24.7 %copy-start.8 = (f32[48,128]{1,0:T(8,128)S(1)}, f32[48,128]{1,0:T(8,128)}, u32[]{:S(2)}) copy-start(f32[48,128]{1,0:T(8,128)} %constant.37.clone.kappa_y) | copy-start | bytes 73732
  24.2 24.7 %copy-start.9 = (bf16[96,96]{1,0:T(8,128)(2,1)S(1)}, bf16[96,96]{1,0:T(8,128)(2,1)}, u32[]{:S(2)}) copy-start(bf16[96,96]{1,0:T(8,128)(2,1)} %constant.33.clone.fwd_low) | copy-start | bytes 55300
  49.3 17.3 %copy-start.1 = (bf16[576,96]{1,0:T(8,128)(2,1)S(1)}, bf16[576,96]{1,0:T(8,128)(2,1)}, u32[]{:S(2)}) copy-start(bf16[576,96]{1,0:T(8,128)(2,1)} %constant.40.clone.low_ref) | copy-start | bytes 331780
  49.4 17.3 %copy-start.2 = (bf16[576,96]{1,0:T(8,128)(2,1)S(1)}, bf16[576,96]{1,0:T(8,128)(2,1)}, u32[]{:S(2)}) copy-start(bf16[576,96]{1,0:T(8,128)(2,1)} %constant.39.clone.high_ref) | copy-start | bytes 331780
  67.8 3.6 %copy-start.15 = (s32[1,1,16,6]{2,1,3,0:T(1,128)S(1)}, s32[1,1,16,6]{2,1,3,0:T(1,128)}, u32[]{:S(2)}) copy-start(s32[1,1,16,6]{2,1,3,0:T(1,128)} %param.23) | copy-start | bytes 1156
  67.8 7.7 %collective-permute-start.1 = (f32[3,4,16,128]{3,2,1,0:T(8,128)S(1)}, f32[3,4,16,128]{3,2,1,0:T(8,128)S(1)}, u32[]{:S(2)}, u32[]{:S(2)}) collective-permute-start(f32[3,4,16,128]{3,2,1,0:T(8,128)S(1)} %bitcast.36), channel_id=1, source_target_pairs={{0,90},{6,0},{12,6},{18,12},{24,18},{30,24},{36,30},{42,36},{48,42... | collective-permute-start | bytes 294920 | tf_op jit(solution)/shard_map/ppermute | solution.py:460
  71.2 4.3 %collective-permute-start = (f32[3,4,16,128]{3,2,1,0:T(8,128)S(1)}, f32[3,4,16,128]{3,2,1,0:T(8,128)S(1)}, u32[]{:S(2)}, u32[]{:S(2)}) collective-permute-start(f32[3,4,16,128]{3,2,1,0:T(8,128)S(1)} %bitcast.37), channel_id=1, source_target_pairs={{0,6},{6,12},{12,18},{18,24},{24,30},{30,36},{36,42},{42,48},{48,5... | collective-permute-start | bytes 294920 | tf_op jit(solution)/shard_map/ppermute | solution.py:460
  71.3 13.5 %all-to-all-start.3 = ((f32[16,9,2,128]{3,2,1,0:T(2,128)}), f32[16,9,2,128]{3,2,1,0:T(2,128)S(1)}, u32[]{:S(2)}, u32[]{:S(2)}) async-start(f32[16,9,2,128]{3,2,1,0:T(2,128)} %bitcast.11), calls=%async_computation.3 | async-start | bytes 294912 | tf_op jit(solution)/shard_map/all_to_all | solution.py:456
  75.5 9.3 %copy-start = (bf16[8,256,256]{2,1,0:T(8,128)(2,1)S(1)}, bf16[8,256,256]{2,1,0:T(8,128)(2,1)}, u32[]{:S(2)}) copy-start(bf16[8,256,256]{2,1,0:T(8,128)(2,1)} %constant.41.clone.table_ref) | copy-start | bytes 3145732
  75.5 9.3 %copy-start.7 = (f32[1,1,16,3,128]{4,2,3,1,0:T(8,128)S(1)}, f32[1,1,16,3,128]{4,2,3,1,0:T(8,128)}, u32[]{:S(2)}) copy-start(f32[1,1,16,3,128]{4,2,3,1,0:T(8,128)} %param.21) | copy-start | bytes 73732
  75.5 9.3 %copy-start.13 = (f32[32,128]{1,0:T(8,128)S(1)}, f32[32,128]{1,0:T(8,128)}, u32[]{:S(2)}) copy-start(f32[32,128]{1,0:T(8,128)} %get-tuple-element.13.live_ref) | copy-start | bytes 49156
